TPU v7x, 256 devices: a whole 4x4x8 slice. The times are simulated.
256 devices in a mesh: batch: 16 (over y, x), proto: 16 (over z, core).
Axes of the slice: x: 4, y: 4, z: 8, core: 2. Of those that a mesh axis runs over, the one named last changes fastest.
Arguments:
- teacher_emb: bfloat16 [256, 8192], P('proto', 'batch'), may hold values from -22 to 22
- student_emb: bfloat16 [256, 8192], P('proto', 'batch'), may hold values from -6 to 6
- prototypes: bfloat16 [256, 65536], P('batch', 'proto'), may hold values from -16 to 16
Outputs:
- grad_proto: float32 [256, 65536], P('batch', 'proto')
- grad_student: float32 [256, 8192], P('proto', 'batch')
- loss: float32 [], replicated
All inputs are finite; a program needn't handle non-finite values.
Results may differ from a plain program's by a relative error of at most 0.00055.
The roundings to bfloat16 on the way count: a program that leaves them out, or rounds other values in their place, can miss the bound.
Values may be sent and summed in bfloat16 or wider, within the bound.
A program may use at most 64 MiB of HBM per device.

v0:
```python
import jax
import jax.numpy as jnp
from jax import lax
from jax.sharding import PartitionSpec as P

ITERS = 3


teacher_temp = 0.07
student_temp = 0.1
epsilon = 1e-06


def unit(matrix):
    values = matrix.astype(jnp.float32)
    factor = lax.rsqrt(jnp.sum(values * values, axis=0, keepdims=True) + epsilon)
    return ((values * factor).astype(jnp.bfloat16), factor)


def cosine(left, right):
    return lax.dot_general(
        left, right, (((0,), (0,)), ((), ())), preferred_element_type=jnp.float32
    )


def shards(teacher_emb, student_emb, prototypes):
    teacher_full, student_full = (
        lax.all_gather(teacher_emb, "proto", axis=0, tiled=True),
        lax.all_gather(student_emb, "proto", axis=0, tiled=True),
    )
    proto_full = lax.all_gather(prototypes, "batch", axis=0, tiled=True)
    proto_unit, proto_scale = unit(proto_full)
    teacher_unit, unused = unit(teacher_full)
    student_unit, student_scale = unit(student_full)
    width = proto_full.shape[0]
    local_rows = teacher_full.shape[1]
    total_rows = local_rows * lax.axis_size("batch")
    expo = jnp.exp(cosine(teacher_unit, proto_unit) / teacher_temp)
    targets = expo
    for iteration in range(ITERS):
        column_total = lax.psum(jnp.sum(targets, axis=0), "batch")
        targets = targets / column_total[None, :]
        row_total = lax.psum(jnp.sum(targets, axis=1), "proto")
        targets = targets / row_total[:, None]
    cos_student = cosine(student_unit, proto_unit)
    logits = cos_student / student_temp
    partial_total = jnp.sum(jnp.exp(logits), axis=1)
    softmax_total = lax.psum(partial_total, "proto")
    logp = logits - jnp.log(softmax_total)[:, None]
    loss_part = -jnp.sum(targets * logp)
    loss = lax.psum(loss_part, ("batch", "proto")) / total_rows
    grad_logit = ((jnp.exp(logp) - targets) / (total_rows * student_temp)).astype(jnp.bfloat16)
    proto_rows = width // lax.axis_size("batch")
    crop_rows = width // lax.axis_size("proto")
    proto_start = lax.axis_index("batch") * proto_rows
    crop_start = lax.axis_index("proto") * crop_rows
    proto_own = lax.dynamic_slice_in_dim(proto_unit, proto_start, proto_rows, 0).astype(jnp.float32)
    student_own = lax.dynamic_slice_in_dim(student_unit, crop_start, crop_rows, 0).astype(
        jnp.float32
    )
    rows = student_unit
    whole_grad = lax.psum(jnp.dot(rows, grad_logit, preferred_element_type=jnp.float32), "batch")
    proto_part = lax.dynamic_slice_in_dim(whole_grad, proto_start, proto_rows, 0)
    rows = proto_unit
    crop_part = lax.psum_scatter(
        lax.dot_general(
            rows, grad_logit, (((1,), (1,)), ((), ())), preferred_element_type=jnp.float32
        ),
        "proto",
        scatter_dimension=0,
        tiled=True,
    )
    proto_dot = lax.psum(jnp.sum(proto_own * proto_part, axis=0), "batch")
    crop_dot = lax.psum(jnp.sum(student_own * crop_part, axis=0), "proto")
    grad_proto = (proto_part - proto_own * proto_dot[None, :]) * proto_scale
    grad_student = (crop_part - student_own * crop_dot[None, :]) * student_scale
    return (grad_proto, grad_student, loss)


def solution(mesh):
    in_specs = (P("proto", "batch"), P("proto", "batch"), P("batch", "proto"))
    out_specs = (P("batch", "proto"), P("proto", "batch"), P())
    return jax.shard_map(shards, mesh=mesh, in_specs=in_specs, out_specs=out_specs, check_vma=False)
```

profile of v0, /device:TPU:2, one launch (start us, length us, event | category | flops | bytes accessed | tf_op | source)
XLA Modules:
  0.0 642.0 jit_solution(15893222598696431938)
XLA Ops:
  7.2 0.0 all-gather.2.cloned.1.call-start
  7.2 0.7 all-gather.2.cloned.1.call-update
  7.9 0.0 reduce-scatter.2.cloned.1.call-start
  7.9 20.9 %all_gather.11 = bf16[256,512]{1,0:T(8,128)(2,1)S(1)} all-gather(bf16[16,512]{1,0:T(8,128)(2,1)} %param.3), channel_id=1, replica_groups=mesh['batch'=16,'proto'=16] {'proto'}, dimensions={0}, use_global_device_ids=true | all-gather | bytes 278528 | tf_op jit(solution)/shard_map/all_gather | solution.py:28
  28.9 15.4 %all_gather.9 = bf16[256,512]{1,0:T(8,128)(2,1)S(1)} all-gather(bf16[16,512]{1,0:T(8,128)(2,1)} %param.4), channel_id=1, replica_groups=mesh['batch'=16,'proto'=16] {'proto'}, dimensions={0}, use_global_device_ids=true | all-gather | bytes 278528 | tf_op jit(solution)/shard_map/all_gather | solution.py:29
  44.3 0.1 fusion.15
  44.4 0.1 fusion.13
  44.5 18.5 %all-gather.2.cloned.1.call-done = bf16[256,4096]{1,0:T(8,128)(2,1)} async-done(((bf16[16,4096]{1,0:T(8,128)(2,1)}), bf16[256,4096]{1,0:T(8,128)(2,1)}) %all-gather.2.cloned.1.call-update) | async-done | bytes 2097168 | tf_op jit(solution)/shard_map/all_gather | solution.py:31
  63.0 2.0 fusion.11
  65.1 2.1 fusion.12
  67.2 4.7 fusion.25
  71.9 67.3 %psum.78 = f32[4096]{0:T(1024)S(1)} all-reduce(f32[4096]{0:T(1024)S(1)} %get-tuple-element.9), channel_id=1, replica_groups=mesh['batch'=16,'proto'=16] {'batch'}, use_global_device_ids=true, to_apply=%region_6.0 | all-reduce | flops 4096 | bytes 32768 | tf_op jit(solution)/shard_map/psum | solution.py:41
  139.2 4.0 divide_reduce_fusion
  143.2 23.5 %psum.79 = f32[512]{0:T(512)S(1)} all-reduce(f32[512]{0:T(512)S(1)} %divide_reduce_fusion), channel_id=1, replica_groups=mesh['batch'=16,'proto'=16] {'proto'}, use_global_device_ids=true, to_apply=%region_8.0 | all-reduce | flops 512 | bytes 4096 | tf_op jit(solution)/shard_map/psum | solution.py:43
  166.8 4.7 fusion.7
  171.5 71.7 %psum.80 = f32[4096]{0:T(1024)S(1)} all-reduce(f32[4096]{0:T(1024)S(1)} %fusion.7), channel_id=1, replica_groups=mesh['batch'=16,'proto'=16] {'batch'}, use_global_device_ids=true, to_apply=%region_10.0 | all-reduce | flops 4096 | bytes 32768 | tf_op jit(solution)/shard_map/psum | solution.py:41
  243.2 4.3 fusion.8
  247.5 23.5 %psum.81 = f32[512]{0:T(512)S(1)} all-reduce(f32[512]{0:T(512)S(1)} %fusion.8), channel_id=1, replica_groups=mesh['batch'=16,'proto'=16] {'proto'}, use_global_device_ids=true, to_apply=%region_12.0 | all-reduce | flops 512 | bytes 4096 | tf_op jit(solution)/shard_map/psum | solution.py:43
  271.0 4.5 fusion.9
  275.5 69.6 %psum.82 = f32[4096]{0:T(1024)S(1)} all-reduce(f32[4096]{0:T(1024)S(1)} %fusion.9), channel_id=1, replica_groups=mesh['batch'=16,'proto'=16] {'batch'}, use_global_device_ids=true, to_apply=%region_14.0 | all-reduce | flops 4096 | bytes 32768 | tf_op jit(solution)/shard_map/psum | solution.py:41
  345.0 4.6 fusion.10
  349.6 4.6 exponential_reduce_fusion
  354.3 23.7 %all-reduce = (f32[512]{0:T(512)S(1)}, f32[512]{0:T(512)S(1)}) all-reduce(f32[512]{0:T(512)S(1)} %get-tuple-element.7, f32[512]{0:T(512)S(1)} %fusion.10), channel_id=1, replica_groups=mesh['batch'=16,'proto'=16] {'proto'}, use_global_device_ids=true, to_apply=%region_3.0 | all-reduce | flops 1024 | bytes 8192 | tf_op jit(solution)/shard_map/psum | solution.py:48
  378.0 9.5 %multiply_reduce_fusion = (f32[]{:T(128)}, bf16[512,4096]{1,0:T(8,128)(2,1)S(1)}) fusion(f32[512,4096]{1,0:T(8,128)} %get-tuple-element.8, f32[512]{0:T(512)S(1)} %log.3, f32[512,4096]{1,0:T(8,128)} %get-tuple-element.10, f32[512]{0:T(512)S(1)} %get-tuple-element.4, f32[4096]{0:T(1024)S(1)} %psum.82, f32[512]{0:T(512)S(1)} %psum.81, f32[4096]{0:T(1024)S(1)} %psum.80, ...), kind=kLoop, calls=%fused_computation.9 | loop fusion | flops 27262976 | bytes 21028868 | tf_op jit(solution)/shard_map/reduce_sum | solution.py:50
  387.5 0.0 copy-start
  387.5 2.0 copy-done
  389.5 2.1 fusion.27
  391.6 0.0 reduce-scatter.2.cloned.1.call-update
  391.6 0.0 all-reduce.3.cloned.1.call-start
  391.7 5.4 fusion.26
  397.0 0.0 all-reduce.3.cloned.1.call-update
  397.7 76.6 %psum.87 = f32[]{:T(128)} all-reduce(f32[]{:T(128)S(6)} %neg.3), channel_id=1, replica_groups=mesh['batch'=16,'proto'=16] {'batch','proto'}, use_global_device_ids=true, to_apply=%region_24.0 | all-reduce | flops 1 | bytes 8 | tf_op jit(solution)/shard_map/psum | solution.py:51
  475.0 0.0 reduce-scatter.2.cloned.1.call-done
  475.0 0.8 fusion.22
  475.8 26.2 %psum.86 = f32[512]{0:T(512)S(1)} all-reduce(f32[512]{0:T(512)S(1)} %fusion.22), channel_id=1, replica_groups=mesh['batch'=16,'proto'=16] {'proto'}, use_global_device_ids=true, to_apply=%region_22.0 | all-reduce | flops 512 | bytes 4096 | tf_op jit(solution)/shard_map/psum | solution.py:74
  502.0 1.4 fusion.24
  503.4 60.9 %all-reduce.3.cloned.1.call-done = f32[256,4096]{1,0:T(8,128)} async-done(((f32[256,4096]{1,0:T(8,128)}), f32[256,4096]{1,0:T(8,128)}) %all-reduce.3.cloned.1.call-update) | async-done | bytes 4194320 | tf_op jit(solution)/shard_map/psum | solution.py:62
  564.4 1.0 fusion.17
  565.4 67.3 %psum.85 = f32[4096]{0:T(1024)S(1)} all-reduce(f32[4096]{0:T(1024)S(1)} %fusion.17), channel_id=1, replica_groups=mesh['batch'=16,'proto'=16] {'batch'}, use_global_device_ids=true, to_apply=%region_19.0 | all-reduce | flops 4096 | bytes 32768 | tf_op jit(solution)/shard_map/psum | solution.py:73
  632.7 1.7 fusion.19
  (5 shorter events, 0.1 us)
Async XLA Ops:
  7.2 55.9 %all-gather.2.cloned.1.call-start = ((), (), s32[]{:S(2)}) async-start(), calls=%async_computation.1 | async-start | bytes 2228224 | tf_op jit(solution)/shard_map/all_gather | solution.py:31
  7.9 467.1 %reduce-scatter.2.cloned.1.call-start = ((), (), s32[]{:S(2)}) async-start(), calls=%async_computation.3 | async-start | bytes 557056 | tf_op jit(solution)/shard_map/reduce_scatter | solution.py:65
  387.5 2.0 copy-start
  391.6 172.7 %all-reduce.3.cloned.1.call-start = ((), (), s32[]{:S(2)}) async-start(), calls=%async_computation.2 | async-start | bytes 8388608 | tf_op jit(solution)/shard_map/psum | solution.py:62
Sparse Core Ops, SparseCore 0:
  10.4 52.5 all-gather.1
  391.7 56.5 reduce-scatter.1
  452.0 112.2 all-reduce.2
where the time goes:
time: 647 us; the launch traced here: 642 us
  blocking collectives  486 us (75%)
  waiting for transfers between devices  80.2 us (12%)
  other arithmetic  40.8 us (6%)
  matrix products  16.9 us (3%)
  between operations  16.2 us (3%)
    psum x3, blocking collectives, shards(): column_total = lax.psum(jnp.sum(targets, axis=0), 'batch')  209 us
    psum x1, blocking collectives, shards(): loss = lax.psum(loss_part, ('batch', 'proto')) / total_rows  76.6 us
    psum x1, blocking collectives, shards(): proto_dot = lax.psum(jnp.sum(proto_own * proto_part, axis=0), 'batch')  67.3 us
    psum x1, waiting for transfers between devices, shards(): lax.psum(jnp.dot(rows, grad_logit, preferred_element_type=jnp.float32), '...  60.9 us
    psum x2, blocking collectives, shards(): row_total = lax.psum(jnp.sum(targets, axis=1), 'proto')  47.1 us
    psum x1, blocking collectives, shards(): crop_dot = lax.psum(jnp.sum(student_own * crop_part, axis=0), 'proto')  26.2 us
    psum x1, blocking collectives, shards(): softmax_total = lax.psum(partial_total, 'proto')  23.7 us
    all_gather x1, blocking collectives, shards(): lax.all_gather(teacher_emb, 'proto', axis=0, tiled=True)  20.9 us
  transfers between devices with their start and end apart: 3, of which 2 were waited for; matrix products, arithmetic and copies ran while one was open for 1% of the time, Pallas kernels for 0%

commit v1 on v0

v1 whole, which is shorter than its diff:
```python
import types

import jax
import jax.numpy as jnp
from jax import lax
from jax.experimental import pallas as pl
from jax.experimental.pallas import tpu as pltpu
from jax.sharding import PartitionSpec as P

F32, BF16 = jnp.float32, jnp.bfloat16
MESH = pl.DeviceIdType.MESH
LOG2E = 1.4426950408889634
TEACHER_TEMP, STUDENT_TEMP, EPS = 0.07, 0.1, 1e-6
K, ROWS, COLS = 256, 512, 4096
CHUNK = 512
NCHUNK = COLS // CHUNK
SIDE = 4
NP = 16
BLK = K // 16
HALF = COLS // 2
QUART = COLS // 4
CROPS = ROWS * SIDE * SIDE
OFFS = (0, -1, 1, 2)
MSGW = CHUNK + 128

SCRATCH = dict(
    praw=((K, COLS), BF16),
    traw=((K, ROWS), BF16),
    sraw=((K, ROWS), BF16),
    tt=((ROWS, K), BF16),
    st=((ROWS, K), BF16),
    su=((K, ROWS), BF16),
    pu=((K, COLS), BF16),
    pscale=((1, COLS), F32),
    sscale=((1, ROWS), F32),
    expo=((ROWS, COLS), F32),
    cos=((ROWS, COLS), F32),
    rowacc=((ROWS, 128), F32),
    colacc=((8, COLS), F32),
    pinv=((8, COLS), F32),
    csb=((ROWS, 128), F32),
    itot=((ROWS, 128), F32),
    tlacc=((8, 128), F32),
    gl=((ROWS, CHUNK), BF16),
    gp=((K, COLS), F32),
    cg=((K, ROWS), F32),
    cgb=((2, 8, BLK, ROWS), F32),
    cgr=((8, BLK, ROWS), F32),
    cgz=((8, BLK, ROWS), F32),
    cgs=((8, BLK, ROWS), F32),
    cx=((4, SIDE, NCHUNK, MSGW), F32),
    cy=((4, SIDE, NCHUNK, MSGW), F32),
    rx=((4, NP, 8, 128), F32),
    lx=((SIDE, 8, 128), F32),
    ly=((SIDE, 8, 128), F32),
    s1=((2, 2, 3, 4 * BLK, QUART), F32),
    r1=((2, 2, 3, 4 * BLK, QUART), F32),
    t1=((2, 4 * BLK, HALF), F32),
    s2=((2, 2, 3, BLK, QUART), F32),
    r2=((2, 2, 3, BLK, QUART), F32),
)
SEMS = dict(
    own=(3,),
    ag_s=(2, 5, 4),
    ag_r=(2, 5, 4),
    ts_s=(2, 16),
    ts_r=(2, 16),
    cx_s=(4, 3),
    cx_r=(4, 3),
    cy_s=(4, 3),
    cy_r=(4, 3),
    rx_s=(4, 15),
    rx_r=(4, 15),
    l_s=(2, 3),
    l_r=(2, 3),
    rs1_s=(2, 2, 3),
    rs1_r=(2, 2, 3),
    rs2_s=(2, 2, 3),
    rs2_r=(2, 2, 3),
    cg_s=(8,),
    cg_r=(8,),
)


def body(t_in, s_in, p_in, gp_out, gs_out, loss_out, *scratch):
    m = types.SimpleNamespace(**dict(zip(list(SCRATCH) + list(SEMS), scratch)))
    bi, pi = lax.axis_index("batch"), lax.axis_index("proto")
    yi, xi = bi // SIDE, bi % SIDE
    zi, ci = pi // 2, pi % 2
    started = []

    def batch_dev(y, x):
        return (y * SIDE + x, pi)

    def proto_dev(p):
        return (bi, p)

    def rdma(src, dst, ssem, rsem, dev):
        return pltpu.make_async_remote_copy(
            src_ref=src, dst_ref=dst, send_sem=ssem, recv_sem=rsem, device_id=dev, device_id_type=MESH
        )

    def send(src, dst, ssem, rsem, dev):
        copy = rdma(src, dst, ssem, rsem, dev)
        copy.start()
        started.append(copy)

    def arrived(dst, ssem, rsem, dev):
        rdma(dst, dst, ssem, rsem, dev).wait_recv()

    barrier = pltpu.get_barrier_semaphore()
    peers = []
    for d in range(1, SIDE):
        peers.append(batch_dev(yi, (xi + d) % SIDE))
        peers.append(batch_dev((yi + d) % SIDE, xi))
    for d in range(1, NP):
        peers.append(proto_dev((pi + d) % NP))
    for peer in peers:
        pl.semaphore_signal(barrier, inc=1, device_id=peer, device_id_type=MESH)
    pl.semaphore_wait(barrier, len(peers))

    def where(h, c1, c2):
        c1, c2 = (c1 + SIDE) % SIDE, (c2 + SIDE) % SIDE
        return (c2, c1) if h == 0 else (c1, c2)

    pos = ((xi, yi), (yi, xi))

    def row0(y, x):
        return pl.multiple_of((y * SIDE + x) * BLK, BLK)

    def piece(h, y, x, part):
        lo, n = ((h * HALF, HALF), (h * HALF, QUART), (h * HALF + QUART, QUART))[part]
        return m.praw.at[pl.ds(row0(y, x), BLK), pl.ds(lo, n)]

    def own_piece(h):
        return p_in.at[:, pl.ds(h * HALF, HALF)]

    own = [
        pltpu.make_async_copy(p_in, m.praw.at[pl.ds(row0(yi, xi), BLK), :], m.own.at[0]),
        pltpu.make_async_copy(t_in, m.traw.at[pl.ds(pl.multiple_of(pi * BLK, BLK), BLK), :], m.own.at[1]),
        pltpu.make_async_copy(s_in, m.sraw.at[pl.ds(pl.multiple_of(pi * BLK, BLK), BLK), :], m.own.at[2]),
    ]

    def put(h, phase, slot, dev_c, blk_c, part, src=None):
        y, x = where(h, *blk_c)
        dst = piece(h, y, x, part)
        send(dst if src is None else src, dst, m.ag_s.at[h, phase, slot], m.ag_r.at[h, phase, slot], batch_dev(*where(h, *dev_c)))

    def got(h, phase, slot, blk_c, part):
        y, x = where(h, *blk_c)
        dst = piece(h, y, x, part)
        arrived(dst, m.ag_s.at[h, phase, slot], m.ag_r.at[h, phase, slot], batch_dev(y, x))

    for h in range(2):
        i1, i2 = pos[h]
        for slot, d in enumerate((1, -1)):
            put(h, 0, slot, (i1 + d, i2), (i1, i2), 0, own_piece(h))
    for h in range(2):
        i1, i2 = pos[h]
        for slot, d in enumerate((1, -1)):
            put(h, 1, slot, (i1, i2 + d), (i1, i2), 0, own_piece(h))

    def ts_rows(ref, p):
        return ref.at[pl.ds(pl.multiple_of(p * BLK, BLK), BLK), :]

    sibling = zi * 2 + 1 - ci
    for d in range(1, 8):
        peer = ((zi + d) % 8) * 2 + ci
        for a, (src, ref) in enumerate(((t_in, m.traw), (s_in, m.sraw))):
            send(src, ts_rows(ref, pi), m.ts_s.at[a, d - 1], m.ts_r.at[a, d - 1], proto_dev(peer))
    for a, (src, ref) in enumerate(((t_in, m.traw), (s_in, m.sraw))):
        send(src, ts_rows(ref, pi), m.ts_s.at[a, 7], m.ts_r.at[a, 7], proto_dev(sibling))
    for copy in own:
        copy.start()

    for slot, d in enumerate((-1, 1)):
        for h in range(2):
            i1, i2 = pos[h]
            got(h, 0, slot, (i1 + d, i2), 0)
            put(h, 0, 2 + slot, (i1 - d, i2), (i1 + d, i2), 1 + slot)
            for s2, d2 in enumerate((1, -1)):
                put(h, 2 + slot, s2, (i1, i2 + d2), (i1 + d, i2), 0)
    for d in range(1, 8):
        peer = ((zi + 8 - d) % 8) * 2 + ci
        for a, ref in enumerate((m.traw, m.sraw)):
            rows = ts_rows(ref, peer)
            arrived(rows, m.ts_s.at[a, d - 1], m.ts_r.at[a, d - 1], proto_dev(peer))
            send(rows, rows, m.ts_s.at[a, 7 + d], m.ts_r.at[a, 7 + d], proto_dev(sibling))
    for h in range(2):
        i1, i2 = pos[h]
        for slot in range(2):
            got(h, 0, 2 + slot, (i1 + 2, i2), 1 + slot)
        for s2, d2 in enumerate((1, -1)):
            put(h, 4, s2, (i1, i2 + d2), (i1 + 2, i2), 0)
    for r, off in enumerate(OFFS):
        for slot, d in enumerate((-1, 1)):
            for h in range(2):
                i1, i2 = pos[h]
                got(h, 1 + r, slot, (i1 + off, i2 + d), 0)
                put(h, 1 + r, 2 + slot, (i1, i2 - d), (i1 + off, i2 + d), 1 + slot)

    for copy in own[1:]:
        copy.wait()
    for a, ref in enumerate((m.traw, m.sraw)):
        arrived(ts_rows(ref, sibling), m.ts_s.at[a, 7], m.ts_r.at[a, 7], proto_dev(sibling))
        for d in range(1, 8):
            rows = ts_rows(ref, ((zi + 8 - d) % 8) * 2 + 1 - ci)
            arrived(rows, m.ts_s.at[a, 7 + d], m.ts_r.at[a, 7 + d], proto_dev(sibling))

    def unit(values):
        values = values.astype(F32)
        factor = lax.rsqrt(jnp.sum(values * values, axis=0, keepdims=True) + EPS)
        return values * factor, factor

    teacher, unused = unit(m.traw[...])
    m.tt[...] = jnp.transpose(teacher).astype(BF16)
    student, factor = unit(m.sraw[...])
    m.sscale[...] = factor
    m.su[...] = student.astype(BF16)
    m.st[...] = jnp.transpose(student).astype(BF16)

    own[0].wait()
    for r, off in enumerate(OFFS):
        for slot in range(2):
            for h in range(2):
                i1, i2 = pos[h]
                got(h, 1 + r, 2 + slot, (i1 + off, i2 + 2), 1 + slot)

    def cols_of(j):
        return pl.ds(pl.multiple_of(j * CHUNK, CHUNK), CHUNK)

    def teacher_chunk(j, carry):
        cols = cols_of(j)
        proto, factor = unit(m.praw[:, cols])
        proto = proto.astype(BF16)
        m.pu[:, cols] = proto
        m.pscale[:, cols] = factor
        c = jnp.dot(m.tt[...], proto, preferred_element_type=F32)
        e = jnp.exp2(c * (LOG2E / TEACHER_TEMP))
        m.expo[:, cols] = e
        m.colacc[:, cols] = jnp.sum(e.reshape(ROWS // 8, 8, CHUNK), axis=0)
        return carry

    def to_message(e):
        for j in range(NCHUNK):
            m.cx[e, xi, j : j + 1, pl.ds(0, CHUNK)] = jnp.sum(
                m.colacc[:, j * CHUNK : (j + 1) * CHUNK], axis=0, keepdims=True
            )

    lax.fori_loop(0, NCHUNK, teacher_chunk, 0)
    to_message(0)

    def ring_send(buf, me, dev, ss, rs):
        for d in range(1, SIDE):
            send(buf.at[me], buf.at[me], ss.at[d - 1], rs.at[d - 1], dev((me + d) % SIDE))

    def ring_sum(buf, me, dev, ss, rs):
        for d in range(1, SIDE):
            frm = (me + SIDE - d) % SIDE
            arrived(buf.at[frm], ss.at[d - 1], rs.at[d - 1], dev(frm))
        return (buf[0] + buf[1]) + (buf[2] + buf[3])

    def along_x(x):
        return batch_dev(yi, x)

    def along_y(y):
        return batch_dev(y, xi)

    def col_start(e):
        ring_send(m.cx.at[e], xi, along_x, m.cx_s.at[e], m.cx_r.at[e])

    def col_finish(e):
        m.cy[e, yi] = ring_sum(m.cx.at[e], xi, along_x, m.cx_s.at[e], m.cx_r.at[e])
        ring_send(m.cy.at[e], yi, along_y, m.cy_s.at[e], m.cy_r.at[e])
        return ring_sum(m.cy.at[e], yi, along_y, m.cy_s.at[e], m.cy_r.at[e])

    def row_start(e):
        for d in range(1, NP):
            send(m.rx.at[e, pi], m.rx.at[e, pi], m.rx_s.at[e, d - 1], m.rx_r.at[e, d - 1], proto_dev((pi + d) % NP))

    def row_finish(e):
        for d in range(1, NP):
            frm = (pi + NP - d) % NP
            arrived(m.rx.at[e, frm], m.rx_s.at[e, d - 1], m.rx_r.at[e, d - 1], proto_dev(frm))
        return jnp.sum(m.rx[e], axis=0)

    def to_rows(acc_ref, e, first):
        for q in range(4):
            block = jnp.transpose(acc_ref[q * 128 : (q + 1) * 128, :])
            m.rx[e, pi, pl.ds(first + q, 1), :] = jnp.sum(block, axis=0, keepdims=True)

    def to_columns(ref, rows):
        for q in range(4):
            ref[q * 128 : (q + 1) * 128, :] = jnp.transpose(jnp.broadcast_to(rows[q : q + 1], (128, 128)))

    m.cx[:, xi, :, pl.ds(CHUNK, 128)] = jnp.zeros((4, NCHUNK, 128), F32)
    col_start(0)

    m.rowacc[...] = jnp.zeros_like(m.rowacc)

    def student_chunk(j, carry):
        cols = cols_of(j)
        c = jnp.dot(m.st[...], m.pu[:, cols], preferred_element_type=F32)
        m.cos[:, cols] = c
        e = jnp.exp2(c * (LOG2E / STUDENT_TEMP))
        m.rowacc[...] += (e[:, 0:128] + e[:, 128:256]) + (e[:, 256:384] + e[:, 384:512])
        return carry

    lax.fori_loop(0, NCHUNK, student_chunk, 0)
    to_rows(m.rowacc, 0, 4)

    def row_pass(e):
        for half in range(2):
            rows = pl.ds(half * 256, 256)

            def step(j, acc):
                for i in range(4):
                    cols = pl.ds(pl.multiple_of(j * CHUNK + i * 128, 128), 128)
                    acc = acc + m.expo[rows, cols].reshape(32, 8, 128) * m.pinv[:, cols]
                return acc

            m.rowacc[rows, :] = lax.fori_loop(0, NCHUNK, step, jnp.zeros((32, 8, 128), F32)).reshape(256, 128)
        to_rows(m.rowacc, e, 0)

    def col_pass(e):
        m.colacc[...] = jnp.zeros_like(m.colacc)

        def step(r, carry):
            rows = pl.ds(pl.multiple_of(r * 64, 64), 64)
            weights = m.csb[rows, :]
            for q in range(COLS // 128):
                cols = slice(q * 128, (q + 1) * 128)
                m.colacc[:, cols] += jnp.sum((m.expo[rows, cols] * weights).reshape(8, 8, 128), axis=0)
            return carry

        lax.fori_loop(0, ROWS // 64, step, 0)
        to_message(e)

    log_total = None
    for e in range(3):
        if e:
            col_pass(e)
            col_start(e)
        total = col_finish(e)[:, :CHUNK]
        total = 1.0 / total
        for j in range(NCHUNK):
            m.pinv[:, j * CHUNK : (j + 1) * CHUNK] = jnp.broadcast_to(total[j : j + 1], (8, CHUNK))
        if e:
            m.rx[e, pi, 4:8, :] = jnp.zeros((4, 128), F32)
        row_pass(e)
        row_start(e)
        rows = row_finish(e)
        to_columns(m.csb, 1.0 / rows[0:4])
        if e == 0:
            to_columns(m.itot, 1.0 / rows[4:8])
            log_total = jnp.sum(jnp.log(rows[4:8]), axis=0, keepdims=True)

    m.tlacc[...] = jnp.zeros_like(m.tlacc)
    m.cg[...] = jnp.zeros_like(m.cg)

    def grad_chunk(j, carry):
        cols = cols_of(j)

        def rows_step(r, inner):
            rows = pl.ds(pl.multiple_of(r * 64, 64), 64)
            weights, inv = m.csb[rows, :], m.itot[rows, :]
            tl = jnp.zeros((64, 128), F32)
            for i in range(4):
                sub = pl.ds(pl.multiple_of(j * CHUNK + i * 128, 128), 128)
                target = (m.expo[rows, sub].reshape(8, 8, 128) * m.pinv[:, sub]).reshape(64, 128) * weights
                c = m.cos[rows, sub]
                prob = jnp.exp2(c * (LOG2E / STUDENT_TEMP)) * inv
                tl = tl + target * c
                m.gl[rows, i * 128 : (i + 1) * 128] = ((prob - target) * (1.0 / (CROPS * STUDENT_TEMP))).astype(BF16)
            m.tlacc[...] += jnp.sum(tl.reshape(8, 8, 128), axis=0)
            return inner

        lax.fori_loop(0, ROWS // 64, rows_step, 0)
        g = m.gl[...]
        proto = m.pu[:, cols]
        part = jnp.dot(m.su[...], g, preferred_element_type=F32)
        m.gp[:, cols] = part
        m.cg[...] += lax.dot_general(proto, g, (((1,), (1,)), ((), ())), preferred_element_type=F32)
        m.colacc[:, cols] = jnp.sum((proto.astype(F32) * part).reshape(K // 8, 8, CHUNK), axis=0)
        return carry

    lax.fori_loop(0, NCHUNK, grad_chunk, 0)
    to_message(3)

    dot_rows = jnp.sum(m.su[...].astype(F32) * m.cg[...], axis=0, keepdims=True)
    for q in range(4):
        m.rx[3, pi, q : q + 1, :] = dot_rows[:, q * 128 : (q + 1) * 128]
    m.rx[3, pi, 4:8, :] = jnp.zeros((4, 128), F32)
    m.rx[3, pi, 4:5, :] = jnp.sum(m.tlacc[...], axis=0, keepdims=True)
    row_start(3)
    col_start(3)
    for p in range(NP):
        m.cgb[p % 2, p // 2] = m.cg[p * BLK : (p + 1) * BLK, :]
    send(m.cgb.at[1 - ci], m.cgr, m.cg_s.at[7], m.cg_r.at[7], proto_dev(sibling))

    def rs_send(s, r, ss, rs, h, axis, direction, slot):
        i1, i2 = pos[h]
        d = 1 - 2 * direction
        dev = (i1 + d, i2) if axis == 0 else (i1, i2 + d)
        send(s.at[h, direction, slot], r.at[h, direction, slot], ss.at[h, direction, slot], rs.at[h, direction, slot], batch_dev(*where(h, *dev)))

    def rs_got(s, r, ss, rs, h, axis, direction, slot):
        i1, i2 = pos[h]
        d = 1 - 2 * direction
        dev = (i1 - d, i2) if axis == 0 else (i1, i2 - d)
        arrived(r.at[h, direction, slot], ss.at[h, direction, slot], rs.at[h, direction, slot], batch_dev(*where(h, *dev)))
        return r[h, direction, slot]

    def reduce_scatter(axis, s, r, ss, rs, load):
        at = [pos[h][axis] for h in range(2)]
        for h in range(2):
            for direction in range(2):
                s[h, direction, 0] = load(h, at[h] + 2, direction)
                rs_send(s, r, ss, rs, h, axis, direction, 0)
        for h in range(2):
            for direction in range(2):
                s[h, direction, 1] = load(h, at[h] + 1 - 2 * direction, 1 - direction)
                rs_send(s, r, ss, rs, h, axis, direction, 1)
        for h in range(2):
            for direction in range(2):
                mine = load(h, at[h] + 1 - 2 * direction, direction)
                s[h, direction, 2] = mine + rs_got(s, r, ss, rs, h, axis, direction, 0)
                rs_send(s, r, ss, rs, h, axis, direction, 2)

    def reduced(axis, s, r, ss, rs, load, h, quarter):
        mine = load(h, pos[h][axis], quarter)
        return mine + rs_got(s, r, ss, rs, h, axis, 1 - quarter, 1) + rs_got(s, r, ss, rs, h, axis, quarter, 2)

    def load1(h, c, quarter):
        c = (c + SIDE) % SIDE
        cols = pl.ds(h * HALF + quarter * QUART, QUART)
        blocks = []
        for u in range(SIDE):
            y, x = (c, u) if h else (u, c)
            blocks.append(m.gp[pl.ds(row0(y, x), BLK), cols])
        return jnp.concatenate(blocks, axis=0)

    def load2(h, c, quarter):
        c = (c + SIDE) % SIDE
        return m.t1[h, pl.ds(pl.multiple_of(c * BLK, BLK), BLK), pl.ds(quarter * QUART, QUART)]

    one = (m.s1, m.r1, m.rs1_s, m.rs1_r)
    two = (m.s2, m.r2, m.rs2_s, m.rs2_r)
    reduce_scatter(0, *one, load1)

    arrived(m.cgr, m.cg_s.at[7], m.cg_r.at[7], proto_dev(sibling))
    m.cgs[...] = m.cgb[ci] + m.cgr[...]
    for d in range(1, 8):
        to = (zi + d) % 8
        send(m.cgs.at[to], m.cgz.at[zi], m.cg_s.at[d - 1], m.cg_r.at[d - 1], proto_dev(to * 2 + ci))
    m.cgz[zi] = m.cgs[zi]

    rows = row_finish(3)
    loss_rows = rows[4:5] * (1.0 / STUDENT_TEMP) - log_total
    m.lx[xi] = jnp.broadcast_to(loss_rows, (8, 128))
    ring_send(m.lx, xi, along_x, m.l_s.at[0], m.l_r.at[0])
    dots = col_finish(3)[:, :CHUNK]
    m.ly[yi] = ring_sum(m.lx, xi, along_x, m.l_s.at[0], m.l_r.at[0])
    ring_send(m.ly, yi, along_y, m.l_s.at[1], m.l_r.at[1])

    for h in range(2):
        for quarter in range(2):
            m.t1[h, :, pl.ds(quarter * QUART, QUART)] = reduced(0, *one, load1, h, quarter)
    reduce_scatter(1, *two, load2)

    loss_out[0, 0] = jnp.sum(ring_sum(m.ly, yi, along_y, m.l_s.at[1], m.l_r.at[1])[0:1]) * (-1.0 / CROPS)
    for d in range(1, 8):
        frm = (zi + 8 - d) % 8
        arrived(m.cgz.at[frm], m.cg_s.at[d - 1], m.cg_r.at[d - 1], proto_dev(frm * 2 + ci))
    crop_part = jnp.sum(m.cgz[...], axis=0)
    student_own = m.su[pl.ds(pl.multiple_of(pi * BLK, BLK), BLK), :].astype(F32)
    for q in range(4):
        cols = slice(q * 128, (q + 1) * 128)
        gs_out[:, cols] = (crop_part[:, cols] - student_own[:, cols] * rows[q : q + 1]) * m.sscale[:, cols]

    for h in range(2):
        for quarter in range(2):
            total = reduced(1, *two, load2, h, quarter)
            for half in range(2):
                j = h * 4 + quarter * 2 + half
                cols = slice(j * CHUNK, (j + 1) * CHUNK)
                proto_own = m.pu[pl.ds(row0(yi, xi), BLK), cols].astype(F32)
                gp_out[:, cols] = (total[:, half * CHUNK : (half + 1) * CHUNK] - proto_own * dots[j : j + 1]) * m.pscale[:, cols]

    for copy in started:
        copy.wait_send()


def shards(teacher_emb, student_emb, prototypes):
    hbm = pl.BlockSpec(memory_space=pl.ANY)
    vmem = pl.BlockSpec(memory_space=pltpu.VMEM)
    grad_proto, grad_student, loss = pl.pallas_call(
        body,
        out_shape=(
            jax.ShapeDtypeStruct((BLK, COLS), F32),
            jax.ShapeDtypeStruct((BLK, ROWS), F32),
            jax.ShapeDtypeStruct((1, 1), F32),
        ),
        in_specs=[hbm] * 3,
        out_specs=(vmem, vmem, pl.BlockSpec(memory_space=pltpu.SMEM)),
        scratch_shapes=[pltpu.VMEM(shape, dtype) for shape, dtype in SCRATCH.values()]
        + [pltpu.SemaphoreType.DMA(shape) for shape in SEMS.values()],
        compiler_params=pltpu.CompilerParams(
            collective_id=0, has_side_effects=True, vmem_limit_bytes=58 * 1024 * 1024
        ),
    )(teacher_emb, student_emb, prototypes)
    return grad_proto, grad_student, loss.reshape(())


def solution(mesh):
    in_specs = (P("proto", "batch"), P("proto", "batch"), P("batch", "proto"))
    out_specs = (P("batch", "proto"), P("proto", "batch"), P())
    return jax.shard_map(shards, mesh=mesh, in_specs=in_specs, out_specs=out_specs, check_vma=False)
```

time: 647 us -> 118 us (0.18)
  blocking collectives: 486 us -> 0 us
  Pallas kernels: 0 us -> 113 us
  waiting for transfers between devices: 80.2 us -> 0 us
  other arithmetic: 40.8 us -> 0 us
  matrix products: 16.9 us -> 0 us
  between operations: 16.2 us -> 2.47 us
    psum x9 -> x0, blocking collectives: 450 us -> none  [the longest x3 209 us: shards(): column_total = lax.psum(jnp.sum(targets, axis=0), 'batch')]
    pallas_call x0 -> x1, Pallas kernels: none -> 113 us  [shards(): pl.pallas_call(body, out_shape=(jax.ShapeDtypeStruct((BLK, COLS), F32), j...]
    psum x1 -> x0, waiting for transfers between devices: 60.9 us -> none  [shards(): lax.psum(jnp.dot(rows, grad_logit, preferred_element_type=jnp.float32), '...]
    all_gather x2 -> x0, blocking collectives: 36.3 us -> none  [the longest x1 20.9 us: shards(): lax.all_gather(teacher_emb, 'proto', axis=0, tiled=True)]
    reduce_sum x11 -> x0, other arithmetic: 35.6 us -> none  [the longest x3 12.9 us: shards(): row_total = lax.psum(jnp.sum(targets, axis=1), 'proto')]
    all_gather x1 -> x0, waiting for transfers between devices: 18.5 us -> none  [shards(): proto_full = lax.all_gather(prototypes, 'batch', axis=0, tiled=True)]
    dot_general x4 -> x0, matrix products: 16.9 us -> none  [the longest x2 9.35 us: cosine(): lax.dot_general(left, right, (((0,), (0,)), ((), ())), preferred_element_...]
  transfers between devices with their start and end apart: 3 -> 0, of which waited for: 2 -> 0; matrix products, arithmetic and copies ran while one was open for 1% -> 0% of each run, Pallas kernels for 0% -> 0%
where the time goes in v1:
time: 118 us
  Pallas kernels  113 us (96%)
  between operations  2.47 us (2%)
  local copies, waits for them, and re-layouts  2.29 us (2%)
    pallas_call x1, Pallas kernels, shards(): pl.pallas_call(body, out_shape=(jax.ShapeDtypeStruct((BLK, COLS), F32), j...  113 us

profile of v1, /device:TPU:2, one launch (start us, length us, event | category | flops | bytes accessed | tf_op | source)
XLA Modules:
  0.0 118.2 jit_solution(16069834319131291876)
XLA Ops:
  0.6 113.4 %shard_map.58 = (f32[16,4096]{1,0:T(8,128)}, f32[16,512]{1,0:T(8,128)}, f32[1,1]{1,0:T(1,128)}) custom-call(bf16[16,512]{1,0:T(8,128)(2,1)} %t_in.1, bf16[16,512]{1,0:T(8,128)(2,1)} %s_in.1, bf16[16,4096]{1,0:T(8,128)(2,1)} %p_in.1), custom_call_target="tpu_custom_call" | custom-call | tf_op jit(solution)/shard_map/pallas_call | solution.py:497
  114.1 0.0 copy-start
  114.1 1.7 %copy.9 = f32[16,4096]{1,0:T(8,128)} copy(f32[16,4096]{1,0:T(8,128)} %get-tuple-element.12) | data formatting | bytes 524288
  115.7 0.0 copy-done
  115.7 0.6 copy.10
Async XLA Ops:
  114.1 1.7 %copy-start = (f32[16,512]{1,0:T(8,128)S(1)}, f32[16,512]{1,0:T(8,128)}, u32[]{:S(2)}) copy-start(f32[16,512]{1,0:T(8,128)} %get-tuple-element.13) | copy-start | bytes 98308

commit v2 on v1

--- a/solution.py
+++ b/solution.py
@@ -53,11 +53,12 @@
     rx=((4, NP, 8, 128), F32),
     lx=((SIDE, 8, 128), F32),
     ly=((SIDE, 8, 128), F32),
-    s1=((2, 2, 3, 4 * BLK, QUART), F32),
-    r1=((2, 2, 3, 4 * BLK, QUART), F32),
+    s1=((2, 2, 3, 4 * BLK, QUART), BF16),
+    r1=((2, 2, 3, 4 * BLK, QUART), BF16),
     t1=((2, 4 * BLK, HALF), F32),
-    s2=((2, 2, 3, BLK, QUART), F32),
-    r2=((2, 2, 3, BLK, QUART), F32),
+    s2=((2, 2, 3, BLK, QUART), BF16),
+    r2=((2, 2, 3, BLK, QUART), BF16),
+    smax=((8, CHUNK), F32),
 )
 SEMS = dict(
     own=(3,),
@@ -297,12 +298,14 @@
     col_start(0)
 
     m.rowacc[...] = jnp.zeros_like(m.rowacc)
+    m.smax[...] = jnp.zeros_like(m.smax)
 
     def student_chunk(j, carry):
         cols = cols_of(j)
         c = jnp.dot(m.st[...], m.pu[:, cols], preferred_element_type=F32)
         m.cos[:, cols] = c
         e = jnp.exp2(c * (LOG2E / STUDENT_TEMP))
+        m.smax[...] = jnp.maximum(m.smax[...], jnp.sum(e.reshape(ROWS // 8, 8, CHUNK), axis=0))
         m.rowacc[...] += (e[:, 0:128] + e[:, 128:256]) + (e[:, 256:384] + e[:, 384:512])
         return carry
 
@@ -341,12 +344,20 @@
         if e:
             col_pass(e)
             col_start(e)
-        total = col_finish(e)[:, :CHUNK]
-        total = 1.0 / total
+        message = col_finish(e)
+        total = message[:, :CHUNK]
+        if e == 1:
+            mass = message[0:2, CHUNK:]
+        if e == 2:
+            growth = jnp.max(total * inverse)
+        inverse = 1.0 / total
         for j in range(NCHUNK):
-            m.pinv[:, j * CHUNK : (j + 1) * CHUNK] = jnp.broadcast_to(total[j : j + 1], (8, CHUNK))
-        if e:
-            m.rx[e, pi, 4:8, :] = jnp.zeros((4, 128), F32)
+            m.pinv[:, j * CHUNK : (j + 1) * CHUNK] = jnp.broadcast_to(inverse[j : j + 1], (8, CHUNK))
+        if e == 1:
+            m.rx[1, pi, 4:8, :] = jnp.zeros((4, 128), F32)
+        if e == 2:
+            m.rx[2, pi, 4:6, :] = jnp.zeros((2, 128), F32) + growth
+            m.rx[2, pi, 6:8, :] = mass
         row_pass(e)
         row_start(e)
         rows = row_finish(e)
@@ -354,6 +365,21 @@
         if e == 0:
             to_columns(m.itot, 1.0 / rows[4:8])
             log_total = jnp.sum(jnp.log(rows[4:8]), axis=0, keepdims=True)
+            bound = jnp.max(jnp.sum(m.smax[...], axis=0, keepdims=True)) * jnp.max(1.0 / rows[4:8])
+            m.cx[1, xi, :, pl.ds(CHUNK, 128)] = jnp.zeros((NCHUNK, 128), F32) + bound
+
+    bound = (jnp.max(m.rx[2][:, 4:6, :]) + jnp.max(m.rx[2][:, 6:8, :])) * (1.05 / (CROPS * STUDENT_TEMP))
+    wire_scale, wire_unscale = 131072.0 / bound, bound * (1.0 / 131072.0)
+
+    def encode(values):
+        values = values * wire_scale
+        square = values * values
+        return ((values * square) * (square * square)).astype(BF16)
+
+    def decode(coded):
+        coded = coded.astype(F32)
+        root = jnp.exp2(jnp.log(jnp.maximum(jnp.abs(coded), 1e-37)) * (-6.0 / 7.0 * LOG2E))
+        return (coded * root) * wire_unscale
 
     m.tlacc[...] = jnp.zeros_like(m.tlacc)
     m.cg[...] = jnp.zeros_like(m.cg)
@@ -384,7 +410,60 @@
         m.colacc[:, cols] = jnp.sum((proto.astype(F32) * part).reshape(K // 8, 8, CHUNK), axis=0)
         return carry
 
-    lax.fori_loop(0, NCHUNK, grad_chunk, 0)
+    def rs_send(lane, h, axis, direction, slot):
+        i1, i2 = pos[h]
+        d = 1 - 2 * direction
+        dev = (i1 + d, i2) if axis == 0 else (i1, i2 + d)
+        src, dst, ss, rs = (r.at[h, direction, slot] for r in lane)
+        send(src, dst, ss, rs, batch_dev(*where(h, *dev)))
+
+    def rs_got(lane, h, axis, direction, slot):
+        i1, i2 = pos[h]
+        d = 1 - 2 * direction
+        dev = (i1 - d, i2) if axis == 0 else (i1, i2 - d)
+        unused, dst, ss, rs = (r.at[h, direction, slot] for r in lane)
+        arrived(dst, ss, rs, batch_dev(*where(h, *dev)))
+        return decode(dst[...])
+
+    def load1(h, c, quarter):
+        c = (c + SIDE) % SIDE
+        cols = pl.ds(h * HALF + quarter * QUART, QUART)
+        blocks = []
+        for u in range(SIDE):
+            y, x = (c, u) if h else (u, c)
+            blocks.append(m.gp[pl.ds(row0(y, x), BLK), cols])
+        return jnp.concatenate(blocks, axis=0)
+
+    def load2(h, c, quarter):
+        c = (c + SIDE) % SIDE
+        return m.t1[h, pl.ds(pl.multiple_of(c * BLK, BLK), BLK), pl.ds(quarter * QUART, QUART)]
+
+    lanes = ((m.s1, m.r1, m.rs1_s, m.rs1_r), (m.s2, m.r2, m.rs2_s, m.rs2_r))
+    loads = (load1, load2)
+
+    def rs_first(axis, h, quarter):
+        at, lane, load = pos[h][axis], lanes[axis], loads[axis]
+        lane[0][h, quarter, 0] = encode(load(h, at + 2, quarter))
+        rs_send(lane, h, axis, quarter, 0)
+        lane[0][h, 1 - quarter, 1] = encode(load(h, at - 1 + 2 * quarter, quarter))
+        rs_send(lane, h, axis, 1 - quarter, 1)
+
+    def rs_second(axis, h, quarter):
+        at, lane, load = pos[h][axis], lanes[axis], loads[axis]
+        lane[0][h, quarter, 2] = encode(load(h, at + 1 - 2 * quarter, quarter) + rs_got(lane, h, axis, quarter, 0))
+        rs_send(lane, h, axis, quarter, 2)
+
+    def rs_third(axis, h, quarter):
+        at, lane, load = pos[h][axis], lanes[axis], loads[axis]
+        return load(h, at, quarter) + rs_got(lane, h, axis, 1 - quarter, 1) + rs_got(lane, h, axis, quarter, 2)
+
+    quarters = ((0, 0), (1, 0), (0, 1), (1, 1))
+    for n, (h, quarter) in enumerate(quarters):
+        first = h * 4 + quarter * 2
+        lax.fori_loop(first, first + 2, grad_chunk, 0)
+        rs_first(0, h, quarter)
+        if n == 2:
+            rs_second(0, *quarters[0])
     to_message(3)
 
     dot_rows = jnp.sum(m.su[...].astype(F32) * m.cg[...], axis=0, keepdims=True)
@@ -398,55 +477,8 @@
         m.cgb[p % 2, p // 2] = m.cg[p * BLK : (p + 1) * BLK, :]
     send(m.cgb.at[1 - ci], m.cgr, m.cg_s.at[7], m.cg_r.at[7], proto_dev(sibling))
 
-    def rs_send(s, r, ss, rs, h, axis, direction, slot):
-        i1, i2 = pos[h]
-        d = 1 - 2 * direction
-        dev = (i1 + d, i2) if axis == 0 else (i1, i2 + d)
-        send(s.at[h, direction, slot], r.at[h, direction, slot], ss.at[h, direction, slot], rs.at[h, direction, slot], batch_dev(*where(h, *dev)))
-
-    def rs_got(s, r, ss, rs, h, axis, direction, slot):
-        i1, i2 = pos[h]
-        d = 1 - 2 * direction
-        dev = (i1 - d, i2) if axis == 0 else (i1, i2 - d)
-        arrived(r.at[h, direction, slot], ss.at[h, direction, slot], rs.at[h, direction, slot], batch_dev(*where(h, *dev)))
-        return r[h, direction, slot]
-
-    def reduce_scatter(axis, s, r, ss, rs, load):
-        at = [pos[h][axis] for h in range(2)]
-        for h in range(2):
-            for direction in range(2):
-                s[h, direction, 0] = load(h, at[h] + 2, direction)
-                rs_send(s, r, ss, rs, h, axis, direction, 0)
-        for h in range(2):
-            for direction in range(2):
-                s[h, direction, 1] = load(h, at[h] + 1 - 2 * direction, 1 - direction)
-                rs_send(s, r, ss, rs, h, axis, direction, 1)
-        for h in range(2):
-            for direction in range(2):
-                mine = load(h, at[h] + 1 - 2 * direction, direction)
-                s[h, direction, 2] = mine + rs_got(s, r, ss, rs, h, axis, direction, 0)
-                rs_send(s, r, ss, rs, h, axis, direction, 2)
-
-    def reduced(axis, s, r, ss, rs, load, h, quarter):
-        mine = load(h, pos[h][axis], quarter)
-        return mine + rs_got(s, r, ss, rs, h, axis, 1 - quarter, 1) + rs_got(s, r, ss, rs, h, axis, quarter, 2)
-
-    def load1(h, c, quarter):
-        c = (c + SIDE) % SIDE
-        cols = pl.ds(h * HALF + quarter * QUART, QUART)
-        blocks = []
-        for u in range(SIDE):
-            y, x = (c, u) if h else (u, c)
-            blocks.append(m.gp[pl.ds(row0(y, x), BLK), cols])
-        return jnp.concatenate(blocks, axis=0)
-
-    def load2(h, c, quarter):
-        c = (c + SIDE) % SIDE
-        return m.t1[h, pl.ds(pl.multiple_of(c * BLK, BLK), BLK), pl.ds(quarter * QUART, QUART)]
-
-    one = (m.s1, m.r1, m.rs1_s, m.rs1_r)
-    two = (m.s2, m.r2, m.rs2_s, m.rs2_r)
-    reduce_scatter(0, *one, load1)
+    for h, quarter in quarters[1:]:
+        rs_second(0, h, quarter)
 
     arrived(m.cgr, m.cg_s.at[7], m.cg_r.at[7], proto_dev(sibling))
     m.cgs[...] = m.cgb[ci] + m.cgr[...]
@@ -463,10 +495,11 @@
     m.ly[yi] = ring_sum(m.lx, xi, along_x, m.l_s.at[0], m.l_r.at[0])
     ring_send(m.ly, yi, along_y, m.l_s.at[1], m.l_r.at[1])
 
-    for h in range(2):
-        for quarter in range(2):
-            m.t1[h, :, pl.ds(quarter * QUART, QUART)] = reduced(0, *one, load1, h, quarter)
-    reduce_scatter(1, *two, load2)
+    for h, quarter in quarters:
+        m.t1[h, :, pl.ds(quarter * QUART, QUART)] = rs_third(0, h, quarter)
+        rs_first(1, h, quarter)
+    for h, quarter in quarters:
+        rs_second(1, h, quarter)
 
     loss_out[0, 0] = jnp.sum(ring_sum(m.ly, yi, along_y, m.l_s.at[1], m.l_r.at[1])[0:1]) * (-1.0 / CROPS)
     for d in range(1, 8):
@@ -478,14 +511,13 @@
         cols = slice(q * 128, (q + 1) * 128)
         gs_out[:, cols] = (crop_part[:, cols] - student_own[:, cols] * rows[q : q + 1]) * m.sscale[:, cols]
 
-    for h in range(2):
-        for quarter in range(2):
-            total = reduced(1, *two, load2, h, quarter)
-            for half in range(2):
-                j = h * 4 + quarter * 2 + half
-                cols = slice(j * CHUNK, (j + 1) * CHUNK)
-                proto_own = m.pu[pl.ds(row0(yi, xi), BLK), cols].astype(F32)
-                gp_out[:, cols] = (total[:, half * CHUNK : (half + 1) * CHUNK] - proto_own * dots[j : j + 1]) * m.pscale[:, cols]
+    for h, quarter in quarters:
+        total = rs_third(1, h, quarter)
+        for half in range(2):
+            j = h * 4 + quarter * 2 + half
+            cols = slice(j * CHUNK, (j + 1) * CHUNK)
+            proto_own = m.pu[pl.ds(row0(yi, xi), BLK), cols].astype(F32)
+            gp_out[:, cols] = (total[:, half * CHUNK : (half + 1) * CHUNK] - proto_own * dots[j : j + 1]) * m.pscale[:, cols]
 
     for copy in started:
         copy.wait_send()

time: 118 us -> 109 us (0.924)
  Pallas kernels: 113 us -> 104 us
    pallas_call x1, Pallas kernels: 113 us -> 104 us  [shards(): pl.pallas_call(body, out_shape=(jax.ShapeDtypeStruct((BLK, COLS), F32), j...]
where the time goes in v2:
time: 109 us; the launch traced here: 108 us
  Pallas kernels  104 us (95%)
  between operations  2.47 us (2%)
  local copies, waits for them, and re-layouts  2.29 us (2%)
    pallas_call x1, Pallas kernels, shards(): pl.pallas_call(body, out_shape=(jax.ShapeDtypeStruct((BLK, COLS), F32), j...  104 us
    unnamed x4, local copies, waits for them, and re-layouts  2.29 us

profile of v2, /device:TPU:2, one launch (start us, length us, event | category | flops | bytes accessed | tf_op | source)
XLA Modules:
  0.0 108.5 jit_solution(5211880454285764568)
XLA Ops:
  0.6 103.7 %shard_map.58 = (f32[16,4096]{1,0:T(8,128)}, f32[16,512]{1,0:T(8,128)}, f32[1,1]{1,0:T(1,128)}) custom-call(bf16[16,512]{1,0:T(8,128)(2,1)} %t_in.1, bf16[16,512]{1,0:T(8,128)(2,1)} %s_in.1, bf16[16,4096]{1,0:T(8,128)(2,1)} %p_in.1), custom_call_target="tpu_custom_call" | custom-call | tf_op jit(solution)/shard_map/pallas_call | solution.py:529
  104.3 0.0 copy-start
  104.3 1.7 %copy.9 = f32[16,4096]{1,0:T(8,128)} copy(f32[16,4096]{1,0:T(8,128)} %get-tuple-element.12) | data formatting | bytes 524288
  106.0 0.0 copy-done
  106.0 0.6 copy.10
Async XLA Ops:
  104.3 1.7 %copy-start = (f32[16,512]{1,0:T(8,128)S(1)}, f32[16,512]{1,0:T(8,128)}, u32[]{:S(2)}) copy-start(f32[16,512]{1,0:T(8,128)} %get-tuple-element.13) | copy-start | bytes 98308

commit v3 on v2

v3 whole, which is shorter than its diff:
```python
import types

import jax
import jax.numpy as jnp
from jax import lax
from jax.experimental import pallas as pl
from jax.experimental.pallas import tpu as pltpu
from jax.sharding import PartitionSpec as P

F32, BF16 = jnp.float32, jnp.bfloat16
MESH = pl.DeviceIdType.MESH
LOG2E = 1.4426950408889634
TEACHER_TEMP, STUDENT_TEMP, EPS = 0.07, 0.1, 1e-6
K, ROWS, COLS = 256, 512, 4096
CHUNK = 512
NCHUNK = COLS // CHUNK
SIDE = 4
NP = 16
BLK = K // 16
QUART = COLS // 4
NEAR = (2, 1, 3)
LAG = 5
CROPS = ROWS * SIDE * SIDE
MSGW = CHUNK + 128

SCRATCH = dict(
    praw=((K, COLS), BF16),
    traw=((K, ROWS), BF16),
    sraw=((K, ROWS), BF16),
    tt=((ROWS, K), BF16),
    st=((ROWS, K), BF16),
    su=((K, ROWS), BF16),
    pu=((K, COLS), BF16),
    pscale=((1, COLS), F32),
    sscale=((1, ROWS), F32),
    expo=((ROWS, COLS), F32),
    cos=((ROWS, COLS), F32),
    rowacc=((ROWS, 128), F32),
    colacc=((8, COLS), F32),
    pinv=((8, COLS), F32),
    csb=((ROWS, 128), F32),
    itot=((ROWS, 128), F32),
    tlacc=((8, 128), F32),
    gl=((ROWS, CHUNK), BF16),
    gp=((K, COLS), F32),
    cg=((K, ROWS), F32),
    cgb=((2, 8, BLK, ROWS), F32),
    cgr=((8, BLK, ROWS), F32),
    cgz=((8, BLK, ROWS), F32),
    cgs=((8, BLK, ROWS), F32),
    cx=((3, SIDE * SIDE, NCHUNK, MSGW), F32),
    dx=((SIDE, NCHUNK, CHUNK), F32),
    dy=((SIDE, NCHUNK, CHUNK), F32),
    rx=((4, NP, 8, 128), F32),
    lx=((SIDE * SIDE, 8, 128), F32),
    s1=((NCHUNK, 3, SIDE * BLK, CHUNK), BF16),
    r1=((NCHUNK, 3, SIDE * BLK, CHUNK), BF16),
    t1=((NCHUNK, SIDE * BLK, CHUNK), F32),
    s2=((NCHUNK, 3, BLK, CHUNK), BF16),
    r2=((NCHUNK, 3, BLK, CHUNK), BF16),
    smax=((8, CHUNK), F32),
)
SEMS = dict(
    own=(3,),
    ag1_s=(4, 3),
    ag1_r=(4, 3),
    ag2_s=(4, 4, 3),
    ag2_r=(4, 4, 3),
    ts_s=(2, 16),
    ts_r=(2, 16),
    cx_s=(3, 15),
    cx_r=(3, 15),
    d_s=(2, 3),
    d_r=(2, 3),
    rx_s=(4, 15),
    rx_r=(4, 15),
    l_s=(15,),
    l_r=(15,),
    rs1_s=(NCHUNK, 3),
    rs1_r=(NCHUNK, 3),
    rs2_s=(NCHUNK, 3),
    rs2_r=(NCHUNK, 3),
    cg_s=(8,),
    cg_r=(8,),
)


def body(t_in, s_in, p_in, gp_out, gs_out, loss_out, *scratch):
    m = types.SimpleNamespace(**dict(zip(list(SCRATCH) + list(SEMS), scratch)))
    bi, pi = lax.axis_index("batch"), lax.axis_index("proto")
    yi, xi = bi // SIDE, bi % SIDE
    zi, ci = pi // 2, pi % 2
    started = []

    def batch_dev(y, x):
        return (y * SIDE + x, pi)

    def proto_dev(p):
        return (bi, p)

    def rdma(src, dst, ssem, rsem, dev):
        return pltpu.make_async_remote_copy(
            src_ref=src, dst_ref=dst, send_sem=ssem, recv_sem=rsem, device_id=dev, device_id_type=MESH
        )

    def send(src, dst, ssem, rsem, dev):
        copy = rdma(src, dst, ssem, rsem, dev)
        copy.start()
        started.append(copy)

    def arrived(dst, ssem, rsem, dev):
        rdma(dst, dst, ssem, rsem, dev).wait_recv()

    barrier = pltpu.get_barrier_semaphore()
    peers = []
    for d in range(1, NP):
        peers.append(((bi + d) % NP, pi))
        peers.append(proto_dev((pi + d) % NP))
    for peer in peers:
        pl.semaphore_signal(barrier, inc=1, device_id=peer, device_id_type=MESH)
    pl.semaphore_wait(barrier, len(peers))

    def where(h, c1, c2):
        c1, c2 = (c1 + SIDE) % SIDE, (c2 + SIDE) % SIDE
        return (c2, c1) if h == 0 else (c1, c2)

    pos = ((xi, yi), (yi, xi))

    def row0(y, x):
        return pl.multiple_of((y * SIDE + x) * BLK, BLK)

    def piece(k, y, x):
        return m.praw.at[pl.ds(row0(y, x), BLK), pl.ds(k * QUART, QUART)]

    own = [
        pltpu.make_async_copy(p_in, m.praw.at[pl.ds(row0(yi, xi), BLK), :], m.own.at[0]),
        pltpu.make_async_copy(t_in, m.traw.at[pl.ds(pl.multiple_of(pi * BLK, BLK), BLK), :], m.own.at[1]),
        pltpu.make_async_copy(s_in, m.sraw.at[pl.ds(pl.multiple_of(pi * BLK, BLK), BLK), :], m.own.at[2]),
    ]

    for k in range(4):
        i1, i2 = pos[k % 2]
        for d in NEAR:
            to = batch_dev(*where(k % 2, i1 + d, i2))
            send(p_in.at[:, pl.ds(k * QUART, QUART)], piece(k, yi, xi), m.ag1_s.at[k, d - 1], m.ag1_r.at[k, d - 1], to)
    for k in range(4):
        i1, i2 = pos[k % 2]
        for d in NEAR:
            to = batch_dev(*where(k % 2, i1, i2 + d))
            send(p_in.at[:, pl.ds(k * QUART, QUART)], piece(k, yi, xi), m.ag2_s.at[k, 0, d - 1], m.ag2_r.at[k, 0, d - 1], to)

    def ts_rows(ref, p):
        return ref.at[pl.ds(pl.multiple_of(p * BLK, BLK), BLK), :]

    sibling = zi * 2 + 1 - ci
    embeddings = ((t_in, m.traw), (s_in, m.sraw))
    for a, (src, ref) in enumerate(embeddings):
        for d in (4, 3, 5, 2, 6, 1, 7):
            peer = ((zi + d) % 8) * 2 + ci
            send(src, ts_rows(ref, pi), m.ts_s.at[a, d - 1], m.ts_r.at[a, d - 1], proto_dev(peer))
        send(src, ts_rows(ref, pi), m.ts_s.at[a, 7], m.ts_r.at[a, 7], proto_dev(sibling))
    for copy in own:
        copy.start()

    for k in range(4):
        h = k % 2
        i1, i2 = pos[h]
        for d in (1, 3, 2):
            y, x = where(h, i1 - d, i2)
            block = piece(k, y, x)
            arrived(block, m.ag1_s.at[k, d - 1], m.ag1_r.at[k, d - 1], batch_dev(y, x))
            for d2 in NEAR:
                send(block, block, m.ag2_s.at[k, d, d2 - 1], m.ag2_r.at[k, d, d2 - 1], batch_dev(*where(h, i1, i2 + d2)))

    def ts_forward(a):
        ref = embeddings[a][1]
        for d in (1, 7, 2, 6, 3, 5, 4):
            peer = ((zi + 8 - d) % 8) * 2 + ci
            rows = ts_rows(ref, peer)
            arrived(rows, m.ts_s.at[a, d - 1], m.ts_r.at[a, d - 1], proto_dev(peer))
            send(rows, rows, m.ts_s.at[a, 7 + d], m.ts_r.at[a, 7 + d], proto_dev(sibling))

    def ts_finish(a):
        ref = embeddings[a][1]
        own[1 + a].wait()
        arrived(ts_rows(ref, sibling), m.ts_s.at[a, 7], m.ts_r.at[a, 7], proto_dev(sibling))
        for d in range(1, 8):
            rows = ts_rows(ref, ((zi + 8 - d) % 8) * 2 + 1 - ci)
            arrived(rows, m.ts_s.at[a, 7 + d], m.ts_r.at[a, 7 + d], proto_dev(sibling))

    ts_forward(0)
    ts_forward(1)

    def unit(values):
        values = values.astype(F32)
        factor = lax.rsqrt(jnp.sum(values * values, axis=0, keepdims=True) + EPS)
        return values * factor, factor

    ts_finish(0)
    teacher, unused = unit(m.traw[...])
    m.tt[...] = jnp.transpose(teacher).astype(BF16)
    ts_finish(1)
    student, factor = unit(m.sraw[...])
    m.sscale[...] = factor
    m.su[...] = student.astype(BF16)
    m.st[...] = jnp.transpose(student).astype(BF16)
    own[0].wait()

    def cols_of(j):
        return pl.ds(j * CHUNK if isinstance(j, int) else pl.multiple_of(j * CHUNK, CHUNK), CHUNK)

    def teacher_chunk(j, carry):
        cols = cols_of(j)
        proto, factor = unit(m.praw[:, cols])
        proto = proto.astype(BF16)
        m.pu[:, cols] = proto
        m.pscale[:, cols] = factor
        c = jnp.dot(m.tt[...], proto, preferred_element_type=F32)
        e = jnp.exp2(c * (LOG2E / TEACHER_TEMP))
        m.expo[:, cols] = e
        m.colacc[:, cols] = jnp.sum(e.reshape(ROWS // 8, 8, CHUNK), axis=0)
        return carry

    def to_message(ref):
        for j in range(NCHUNK):
            ref[j : j + 1, pl.ds(0, CHUNK)] = jnp.sum(m.colacc[:, j * CHUNK : (j + 1) * CHUNK], axis=0, keepdims=True)

    for k in range(4):
        h = k % 2
        i1, i2 = pos[h]
        for r in range(4):
            for d in (1, 3, 2):
                y, x = where(h, i1 - r, i2 - d)
                arrived(piece(k, y, x), m.ag2_s.at[k, r, d - 1], m.ag2_r.at[k, r, d - 1], batch_dev(y, x))
        lax.fori_loop(2 * k, 2 * k + 2, teacher_chunk, 0)
    to_message(m.cx.at[0, bi])

    def all_send(buf, ss, rs):
        for d in range(1, NP):
            send(buf.at[bi], buf.at[bi], ss.at[d - 1], rs.at[d - 1], ((bi + d) % NP, pi))

    def all_sum(buf, ss, rs):
        for d in range(1, NP):
            frm = (bi + NP - d) % NP
            arrived(buf.at[frm], ss.at[d - 1], rs.at[d - 1], (frm, pi))
        return jnp.sum(buf[...], axis=0)

    def message(e):
        return m.cx.at[e] if e == 1 else m.cx.at[e, :, :, pl.ds(0, CHUNK)]

    def col_start(e):
        all_send(message(e), m.cx_s.at[e], m.cx_r.at[e])

    def col_finish(e):
        return all_sum(message(e), m.cx_s.at[e], m.cx_r.at[e])

    def ring_send(buf, me, dev, ss, rs):
        for d in NEAR:
            send(buf.at[me], buf.at[me], ss.at[d - 1], rs.at[d - 1], dev((me + d) % SIDE))

    def ring_sum(buf, me, dev, ss, rs):
        for d in range(1, SIDE):
            frm = (me + SIDE - d) % SIDE
            arrived(buf.at[frm], ss.at[d - 1], rs.at[d - 1], dev(frm))
        return (buf[0] + buf[1]) + (buf[2] + buf[3])

    def along_x(x):
        return batch_dev(yi, x)

    def along_y(y):
        return batch_dev(y, xi)

    def row_start(e):
        for d in range(1, NP):
            send(m.rx.at[e, pi], m.rx.at[e, pi], m.rx_s.at[e, d - 1], m.rx_r.at[e, d - 1], proto_dev((pi + d) % NP))

    def row_finish(e):
        for d in range(1, NP):
            frm = (pi + NP - d) % NP
            arrived(m.rx.at[e, frm], m.rx_s.at[e, d - 1], m.rx_r.at[e, d - 1], proto_dev(frm))
        return jnp.sum(m.rx[e], axis=0)

    def to_rows(acc_ref, e, first):
        for q in range(4):
            block = jnp.transpose(acc_ref[q * 128 : (q + 1) * 128, :])
            m.rx[e, pi, pl.ds(first + q, 1), :] = jnp.sum(block, axis=0, keepdims=True)

    def to_columns(ref, rows):
        for q in range(4):
            ref[q * 128 : (q + 1) * 128, :] = jnp.transpose(jnp.broadcast_to(rows[q : q + 1], (128, 128)))

    col_start(0)

    m.rowacc[...] = jnp.zeros_like(m.rowacc)
    m.smax[...] = jnp.zeros_like(m.smax)

    def student_chunk(j, carry):
        cols = cols_of(j)
        c = jnp.dot(m.st[...], m.pu[:, cols], preferred_element_type=F32)
        m.cos[:, cols] = c
        e = jnp.exp2(c * (LOG2E / STUDENT_TEMP))
        m.smax[...] = jnp.maximum(m.smax[...], jnp.sum(e.reshape(ROWS // 8, 8, CHUNK), axis=0))
        m.rowacc[...] += (e[:, 0:128] + e[:, 128:256]) + (e[:, 256:384] + e[:, 384:512])
        return carry

    lax.fori_loop(0, NCHUNK, student_chunk, 0)
    to_rows(m.rowacc, 0, 4)

    def row_pass(e):
        for half in range(2):
            rows = pl.ds(half * 256, 256)

            def step(j, acc):
                for i in range(4):
                    cols = pl.ds(pl.multiple_of(j * CHUNK + i * 128, 128), 128)
                    acc = acc + m.expo[rows, cols].reshape(32, 8, 128) * m.pinv[:, cols]
                return acc

            m.rowacc[rows, :] = lax.fori_loop(0, NCHUNK, step, jnp.zeros((32, 8, 128), F32)).reshape(256, 128)
        to_rows(m.rowacc, e, 0)

    def col_pass(e):
        m.colacc[...] = jnp.zeros_like(m.colacc)

        def step(r, carry):
            rows = pl.ds(pl.multiple_of(r * 64, 64), 64)
            weights = m.csb[rows, :]
            for q in range(COLS // 128):
                cols = slice(q * 128, (q + 1) * 128)
                m.colacc[:, cols] += jnp.sum((m.expo[rows, cols] * weights).reshape(8, 8, 128), axis=0)
            return carry

        lax.fori_loop(0, ROWS // 64, step, 0)
        to_message(m.cx.at[e, bi])

    log_total = None
    for e in range(3):
        if e:
            col_pass(e)
            col_start(e)
        sums = col_finish(e)
        total = sums[:, :CHUNK]
        if e == 1:
            mass = sums[0:2, CHUNK:]
        if e == 2:
            growth = jnp.max(total * inverse)
        inverse = 1.0 / total
        for j in range(NCHUNK):
            m.pinv[:, j * CHUNK : (j + 1) * CHUNK] = jnp.broadcast_to(inverse[j : j + 1], (8, CHUNK))
        if e == 1:
            m.rx[1, pi, 4:8, :] = jnp.zeros((4, 128), F32)
        if e == 2:
            m.rx[2, pi, 4:6, :] = jnp.zeros((2, 128), F32) + growth
            m.rx[2, pi, 6:8, :] = mass
        row_pass(e)
        row_start(e)
        rows = row_finish(e)
        to_columns(m.csb, 1.0 / rows[0:4])
        if e == 0:
            to_columns(m.itot, 1.0 / rows[4:8])
            log_total = jnp.sum(jnp.log(rows[4:8]), axis=0, keepdims=True)
            bound = jnp.max(jnp.sum(m.smax[...], axis=0, keepdims=True)) * jnp.max(1.0 / rows[4:8])
            m.cx[1, bi, :, pl.ds(CHUNK, 128)] = jnp.zeros((NCHUNK, 128), F32) + bound

    bound = (jnp.max(m.rx[2][:, 4:6, :]) + jnp.max(m.rx[2][:, 6:8, :])) * (1.05 / (CROPS * STUDENT_TEMP))
    wire_scale, wire_unscale = 8192.0 / bound, bound * (1.0 / 8192.0)

    def encode(values):
        values = values * wire_scale
        square = values * values
        e8 = square * square
        return (values * (e8 * e8)).astype(BF16)

    def decode(coded):
        coded = coded.astype(F32)
        root = jnp.exp2(jnp.log(jnp.maximum(jnp.abs(coded), 1e-37)) * (-8.0 / 9.0 * LOG2E))
        return (coded * root) * wire_unscale

    m.tlacc[...] = jnp.zeros_like(m.tlacc)
    m.cg[...] = jnp.zeros_like(m.cg)

    def grad_chunk(j, carry):
        cols = cols_of(j)

        def rows_step(r, inner):
            rows = pl.ds(pl.multiple_of(r * 64, 64), 64)
            weights, inv = m.csb[rows, :], m.itot[rows, :]
            tl = jnp.zeros((64, 128), F32)
            for i in range(4):
                sub = pl.ds(j * CHUNK + i * 128, 128)
                target = (m.expo[rows, sub].reshape(8, 8, 128) * m.pinv[:, sub]).reshape(64, 128) * weights
                c = m.cos[rows, sub]
                prob = jnp.exp2(c * (LOG2E / STUDENT_TEMP)) * inv
                tl = tl + target * c
                m.gl[rows, i * 128 : (i + 1) * 128] = ((prob - target) * (1.0 / (CROPS * STUDENT_TEMP))).astype(BF16)
            m.tlacc[...] += jnp.sum(tl.reshape(8, 8, 128), axis=0)
            return inner

        lax.fori_loop(0, ROWS // 64, rows_step, 0)
        g = m.gl[...]
        proto = m.pu[:, cols]
        part = jnp.dot(m.su[...], g, preferred_element_type=F32)
        m.gp[:, cols] = part
        m.cg[...] += lax.dot_general(proto, g, (((1,), (1,)), ((), ())), preferred_element_type=F32)
        m.colacc[:, cols] = jnp.sum((proto.astype(F32) * part).reshape(K // 8, 8, CHUNK), axis=0)
        return carry

    def first_rows(h, c, cols):
        c = (c + SIDE) % SIDE
        blocks = []
        for u in range(SIDE):
            y, x = (c, u) if h else (u, c)
            blocks.append(m.gp[pl.ds(row0(y, x), BLK), cols])
        return jnp.concatenate(blocks, axis=0)

    def second_rows(j, c):
        return m.t1[j, pl.ds(pl.multiple_of(((c + SIDE) % SIDE) * BLK, BLK), BLK), :]

    def first_send(j):
        h = j % 2
        i1, i2 = pos[h]
        for d in NEAR:
            m.s1[j, d - 1] = encode(first_rows(h, i1 + d, slice(j * CHUNK, (j + 1) * CHUNK)))
            to = batch_dev(*where(h, i1 + d, i2))
            send(m.s1.at[j, d - 1], m.r1.at[j, d - 1], m.rs1_s.at[j, d - 1], m.rs1_r.at[j, d - 1], to)

    def second_send(j):
        h = j % 2
        i1, i2 = pos[h]
        total = first_rows(h, i1, slice(j * CHUNK, (j + 1) * CHUNK))
        for d in range(1, SIDE):
            arrived(m.r1.at[j, d - 1], m.rs1_s.at[j, d - 1], m.rs1_r.at[j, d - 1], batch_dev(*where(h, i1 - d, i2)))
            total = total + decode(m.r1[j, d - 1])
        m.t1[j] = total
        for d in NEAR:
            m.s2[j, d - 1] = encode(second_rows(j, i2 + d))
            to = batch_dev(*where(h, i1, i2 + d))
            send(m.s2.at[j, d - 1], m.r2.at[j, d - 1], m.rs2_s.at[j, d - 1], m.rs2_r.at[j, d - 1], to)

    def reduced(j):
        h = j % 2
        i1, i2 = pos[h]
        total = second_rows(j, i2)
        for d in range(1, SIDE):
            arrived(m.r2.at[j, d - 1], m.rs2_s.at[j, d - 1], m.rs2_r.at[j, d - 1], batch_dev(*where(h, i1, i2 - d)))
            total = total + decode(m.r2[j, d - 1])
        return total

    for j in range(NCHUNK):
        grad_chunk(j, 0)
        first_send(j)
        if j >= LAG:
            second_send(j - LAG)
    for p in range(NP):
        m.cgb[p % 2, p // 2] = m.cg[p * BLK : (p + 1) * BLK, :]
    send(m.cgb.at[1 - ci], m.cgr, m.cg_s.at[7], m.cg_r.at[7], proto_dev(sibling))
    dot_rows = jnp.sum(m.su[...].astype(F32) * m.cg[...], axis=0, keepdims=True)
    for q in range(4):
        m.rx[3, pi, q : q + 1, :] = dot_rows[:, q * 128 : (q + 1) * 128]
    m.rx[3, pi, 4:8, :] = jnp.zeros((4, 128), F32)
    m.rx[3, pi, 4:5, :] = jnp.sum(m.tlacc[...], axis=0, keepdims=True)
    row_start(3)
    to_message(m.dx.at[xi])
    ring_send(m.dx, xi, along_x, m.d_s.at[0], m.d_r.at[0])

    arrived(m.cgr, m.cg_s.at[7], m.cg_r.at[7], proto_dev(sibling))
    m.cgs[...] = m.cgb[ci] + m.cgr[...]
    for d in range(1, 8):
        to = (zi + d) % 8
        send(m.cgs.at[to], m.cgz.at[zi], m.cg_s.at[d - 1], m.cg_r.at[d - 1], proto_dev(to * 2 + ci))
    m.cgz[zi] = m.cgs[zi]

    second_send(NCHUNK - LAG)
    m.dy[yi] = ring_sum(m.dx, xi, along_x, m.d_s.at[0], m.d_r.at[0])
    ring_send(m.dy, yi, along_y, m.d_s.at[1], m.d_r.at[1])
    second_send(NCHUNK - LAG + 1)

    rows = row_finish(3)
    loss_rows = rows[4:5] * (1.0 / STUDENT_TEMP) - log_total
    m.lx[bi] = jnp.broadcast_to(loss_rows, (8, 128))
    all_send(m.lx, m.l_s, m.l_r)
    for j in range(NCHUNK - LAG + 2, NCHUNK):
        second_send(j)
    dots = ring_sum(m.dy, yi, along_y, m.d_s.at[1], m.d_r.at[1])

    loss_out[0, 0] = jnp.sum(all_sum(m.lx, m.l_s, m.l_r)[0:1]) * (-1.0 / CROPS)
    for d in range(1, 8):
        frm = (zi + 8 - d) % 8
        arrived(m.cgz.at[frm], m.cg_s.at[d - 1], m.cg_r.at[d - 1], proto_dev(frm * 2 + ci))
    crop_part = jnp.sum(m.cgz[...], axis=0)
    student_own = m.su[pl.ds(pl.multiple_of(pi * BLK, BLK), BLK), :].astype(F32)
    for q in range(4):
        cols = slice(q * 128, (q + 1) * 128)
        gs_out[:, cols] = (crop_part[:, cols] - student_own[:, cols] * rows[q : q + 1]) * m.sscale[:, cols]

    proto_rows = pl.ds(row0(yi, xi), BLK)
    for j in range(NCHUNK):
        cols = slice(j * CHUNK, (j + 1) * CHUNK)
        proto_own = m.pu[proto_rows, cols].astype(F32)
        gp_out[:, cols] = (reduced(j) - proto_own * dots[j : j + 1]) * m.pscale[:, cols]

    for copy in started:
        copy.wait_send()


def shards(teacher_emb, student_emb, prototypes):
    hbm = pl.BlockSpec(memory_space=pl.ANY)
    vmem = pl.BlockSpec(memory_space=pltpu.VMEM)
    grad_proto, grad_student, loss = pl.pallas_call(
        body,
        out_shape=(
            jax.ShapeDtypeStruct((BLK, COLS), F32),
            jax.ShapeDtypeStruct((BLK, ROWS), F32),
            jax.ShapeDtypeStruct((1, 1), F32),
        ),
        in_specs=[hbm] * 3,
        out_specs=(vmem, vmem, pl.BlockSpec(memory_space=pltpu.SMEM)),
        scratch_shapes=[pltpu.VMEM(shape, dtype) for shape, dtype in SCRATCH.values()]
        + [pltpu.SemaphoreType.DMA(shape) for shape in SEMS.values()],
        compiler_params=pltpu.CompilerParams(
            collective_id=0, has_side_effects=True, vmem_limit_bytes=58 * 1024 * 1024
        ),
    )(teacher_emb, student_emb, prototypes)
    return grad_proto, grad_student, loss.reshape(())


def solution(mesh):
    in_specs = (P("proto", "batch"), P("proto", "batch"), P("batch", "proto"))
    out_specs = (P("batch", "proto"), P("proto", "batch"), P())
    return jax.shard_map(shards, mesh=mesh, in_specs=in_specs, out_specs=out_specs, check_vma=False)
```

time: 109 us -> 102 us (0.936)
  Pallas kernels: 104 us -> 95.9 us
    pallas_call x1, Pallas kernels: 104 us -> 95.9 us  [shards(): pl.pallas_call(body, out_shape=(jax.ShapeDtypeStruct((BLK, COLS), F32), j...]
where the time goes in v3:
time: 102 us; the launch traced here: 101 us
  Pallas kernels  95.9 us (94%)
  between operations  2.47 us (2%)
  local copies, waits for them, and re-layouts  2.29 us (2%)
    pallas_call x1, Pallas kernels, shards(): pl.pallas_call(body, out_shape=(jax.ShapeDtypeStruct((BLK, COLS), F32), j...  95.9 us
    unnamed x4, local copies, waits for them, and re-layouts  2.29 us

profile of v3, /device:TPU:2, one launch (start us, length us, event | category | flops | bytes accessed | tf_op | source)
XLA Modules:
  0.0 100.6 jit_solution(5242755462396504891)
XLA Ops:
  0.6 95.9 %shard_map.58 = (f32[16,4096]{1,0:T(8,128)}, f32[16,512]{1,0:T(8,128)}, f32[1,1]{1,0:T(1,128)}) custom-call(bf16[16,512]{1,0:T(8,128)(2,1)} %t_in.1, bf16[16,512]{1,0:T(8,128)(2,1)} %s_in.1, bf16[16,4096]{1,0:T(8,128)(2,1)} %p_in.1), custom_call_target="tpu_custom_call" | custom-call | tf_op jit(solution)/shard_map/pallas_call | solution.py:509
  96.5 0.0 copy-start
  96.5 1.7 %copy.9 = f32[16,4096]{1,0:T(8,128)} copy(f32[16,4096]{1,0:T(8,128)} %get-tuple-element.12) | data formatting | bytes 524288
  98.2 0.0 copy-done
  98.2 0.6 copy.10
Async XLA Ops:
  96.5 1.7 %copy-start = (f32[16,512]{1,0:T(8,128)S(1)}, f32[16,512]{1,0:T(8,128)}, u32[]{:S(2)}) copy-start(f32[16,512]{1,0:T(8,128)} %get-tuple-element.13) | copy-start | bytes 98308

commit v4 on v3

--- a/solution.py
+++ b/solution.py
@@ -21,6 +21,8 @@
 NEAR = (2, 1, 3)
 LAG = 5
 CROPS = ROWS * SIDE * SIDE
+WIRE_TOP = 8192.0
+CROP_SCALE = WIRE_TOP * (CROPS * STUDENT_TEMP) / 2.1
 MSGW = CHUNK + 128
 
 SCRATCH = dict(
@@ -46,8 +48,9 @@
     cg=((K, ROWS), F32),
     cgb=((2, 8, BLK, ROWS), F32),
     cgr=((8, BLK, ROWS), F32),
-    cgz=((8, BLK, ROWS), F32),
-    cgs=((8, BLK, ROWS), F32),
+    cgz=((8, BLK, ROWS), BF16),
+    cgs=((8, BLK, ROWS), BF16),
+    cgm=((8, BLK, ROWS), F32),
     cx=((3, SIDE * SIDE, NCHUNK, MSGW), F32),
     dx=((SIDE, NCHUNK, CHUNK), F32),
     dy=((SIDE, NCHUNK, CHUNK), F32),
@@ -113,9 +116,10 @@
 
     barrier = pltpu.get_barrier_semaphore()
     peers = []
-    for d in range(1, NP):
+    for d in (8, 9, 7, 6, 10, 11, 5, 4, 12, 13, 3, 2, 14, 15, 1):
+        peers.append(proto_dev((pi + d) % NP))
+    for d in (10, 9, 11, 6, 14, 8, 2, 5, 7, 13, 15, 1, 3, 4, 12):
         peers.append(((bi + d) % NP, pi))
-        peers.append(proto_dev((pi + d) % NP))
     for peer in peers:
         pl.semaphore_signal(barrier, inc=1, device_id=peer, device_id_type=MESH)
     pl.semaphore_wait(barrier, len(peers))
@@ -307,16 +311,16 @@
     to_rows(m.rowacc, 0, 4)
 
     def row_pass(e):
-        for half in range(2):
-            rows = pl.ds(half * 256, 256)
-
-            def step(j, acc):
-                for i in range(4):
-                    cols = pl.ds(pl.multiple_of(j * CHUNK + i * 128, 128), 128)
-                    acc = acc + m.expo[rows, cols].reshape(32, 8, 128) * m.pinv[:, cols]
-                return acc
-
-            m.rowacc[rows, :] = lax.fori_loop(0, NCHUNK, step, jnp.zeros((32, 8, 128), F32)).reshape(256, 128)
+        def step(r, carry):
+            rows = pl.ds(pl.multiple_of(r * 64, 64), 64)
+            acc = jnp.zeros((8, 8, 128), F32)
+            for q in range(COLS // 128):
+                cols = slice(q * 128, (q + 1) * 128)
+                acc = acc + m.expo[rows, cols].reshape(8, 8, 128) * m.pinv[:, cols]
+            m.rowacc[rows, :] = acc.reshape(64, 128)
+            return carry
+
+        lax.fori_loop(0, ROWS // 64, step, 0)
         to_rows(m.rowacc, e, 0)
 
     def col_pass(e):
@@ -363,18 +367,18 @@
             m.cx[1, bi, :, pl.ds(CHUNK, 128)] = jnp.zeros((NCHUNK, 128), F32) + bound
 
     bound = (jnp.max(m.rx[2][:, 4:6, :]) + jnp.max(m.rx[2][:, 6:8, :])) * (1.05 / (CROPS * STUDENT_TEMP))
-    wire_scale, wire_unscale = 8192.0 / bound, bound * (1.0 / 8192.0)
-
-    def encode(values):
-        values = values * wire_scale
+    wire_scale, wire_unscale = WIRE_TOP / bound, bound * (1.0 / WIRE_TOP)
+
+    def encode(values, scale):
+        values = values * scale
         square = values * values
         e8 = square * square
         return (values * (e8 * e8)).astype(BF16)
 
-    def decode(coded):
+    def decode(coded, unscale):
         coded = coded.astype(F32)
         root = jnp.exp2(jnp.log(jnp.maximum(jnp.abs(coded), 1e-37)) * (-8.0 / 9.0 * LOG2E))
-        return (coded * root) * wire_unscale
+        return (coded * root) * unscale
 
     m.tlacc[...] = jnp.zeros_like(m.tlacc)
     m.cg[...] = jnp.zeros_like(m.cg)
@@ -420,7 +424,7 @@
         h = j % 2
         i1, i2 = pos[h]
         for d in NEAR:
-            m.s1[j, d - 1] = encode(first_rows(h, i1 + d, slice(j * CHUNK, (j + 1) * CHUNK)))
+            m.s1[j, d - 1] = encode(first_rows(h, i1 + d, slice(j * CHUNK, (j + 1) * CHUNK)), wire_scale)
             to = batch_dev(*where(h, i1 + d, i2))
             send(m.s1.at[j, d - 1], m.r1.at[j, d - 1], m.rs1_s.at[j, d - 1], m.rs1_r.at[j, d - 1], to)
 
@@ -430,10 +434,10 @@
         total = first_rows(h, i1, slice(j * CHUNK, (j + 1) * CHUNK))
         for d in range(1, SIDE):
             arrived(m.r1.at[j, d - 1], m.rs1_s.at[j, d - 1], m.rs1_r.at[j, d - 1], batch_dev(*where(h, i1 - d, i2)))
-            total = total + decode(m.r1[j, d - 1])
+            total = total + decode(m.r1[j, d - 1], wire_unscale)
         m.t1[j] = total
         for d in NEAR:
-            m.s2[j, d - 1] = encode(second_rows(j, i2 + d))
+            m.s2[j, d - 1] = encode(second_rows(j, i2 + d), wire_scale)
             to = batch_dev(*where(h, i1, i2 + d))
             send(m.s2.at[j, d - 1], m.r2.at[j, d - 1], m.rs2_s.at[j, d - 1], m.rs2_r.at[j, d - 1], to)
 
@@ -443,7 +447,7 @@
         total = second_rows(j, i2)
         for d in range(1, SIDE):
             arrived(m.r2.at[j, d - 1], m.rs2_s.at[j, d - 1], m.rs2_r.at[j, d - 1], batch_dev(*where(h, i1, i2 - d)))
-            total = total + decode(m.r2[j, d - 1])
+            total = total + decode(m.r2[j, d - 1], wire_unscale)
         return total
 
     for j in range(NCHUNK):
@@ -464,11 +468,11 @@
     ring_send(m.dx, xi, along_x, m.d_s.at[0], m.d_r.at[0])
 
     arrived(m.cgr, m.cg_s.at[7], m.cg_r.at[7], proto_dev(sibling))
-    m.cgs[...] = m.cgb[ci] + m.cgr[...]
+    m.cgm[...] = m.cgb[ci] + m.cgr[...]
+    m.cgs[...] = encode(m.cgm[...], CROP_SCALE)
     for d in range(1, 8):
         to = (zi + d) % 8
         send(m.cgs.at[to], m.cgz.at[zi], m.cg_s.at[d - 1], m.cg_r.at[d - 1], proto_dev(to * 2 + ci))
-    m.cgz[zi] = m.cgs[zi]
 
     second_send(NCHUNK - LAG)
     m.dy[yi] = ring_sum(m.dx, xi, along_x, m.d_s.at[0], m.d_r.at[0])
@@ -484,10 +488,11 @@
     dots = ring_sum(m.dy, yi, along_y, m.d_s.at[1], m.d_r.at[1])
 
     loss_out[0, 0] = jnp.sum(all_sum(m.lx, m.l_s, m.l_r)[0:1]) * (-1.0 / CROPS)
+    crop_part = m.cgm[zi]
     for d in range(1, 8):
         frm = (zi + 8 - d) % 8
         arrived(m.cgz.at[frm], m.cg_s.at[d - 1], m.cg_r.at[d - 1], proto_dev(frm * 2 + ci))
-    crop_part = jnp.sum(m.cgz[...], axis=0)
+        crop_part = crop_part + decode(m.cgz[frm], 1.0 / CROP_SCALE)
     student_own = m.su[pl.ds(pl.multiple_of(pi * BLK, BLK), BLK), :].astype(F32)
     for q in range(4):
         cols = slice(q * 128, (q + 1) * 128)
@@ -509,8 +514,8 @@
     grad_proto, grad_student, loss = pl.pallas_call(
         body,
         out_shape=(
-            jax.ShapeDtypeStruct((BLK, COLS), F32),
-            jax.ShapeDtypeStruct((BLK, ROWS), F32),
+            pltpu.VMEM((BLK, COLS), F32),
+            pltpu.VMEM((BLK, ROWS), F32),
             jax.ShapeDtypeStruct((1, 1), F32),
         ),
         in_specs=[hbm] * 3,

time: 102 us -> 97.5 us (0.956)
  Pallas kernels: 95.9 us -> 93.1 us
    pallas_call x1, Pallas kernels: 95.9 us -> 93.1 us  [shards(): pl.pallas_call(body, out_shape=(pltpu.VMEM((BLK, COLS), F32), pltpu.VMEM(...]
    unnamed x4 -> x2, local copies, waits for them, and re-layouts: 2.29 us -> 1.32 us
where the time goes in v4:
time: 97.5 us; the launch traced here: 96.7 us
  Pallas kernels  93.1 us (95%)
  between operations  2.33 us (2%)
  local copies, waits for them, and re-layouts  1.32 us (1%)
    pallas_call x1, Pallas kernels, shards(): pl.pallas_call(body, out_shape=(pltpu.VMEM((BLK, COLS), F32), pltpu.VMEM(...  93.1 us

profile of v4, /device:TPU:2, one launch (start us, length us, event | category | flops | bytes accessed | tf_op | source)
XLA Modules:
  0.0 96.7 jit_solution(10995690707125663925)
XLA Ops:
  0.6 93.1 %shard_map.58 = (f32[16,4096]{1,0:T(8,128)S(1)}, f32[16,512]{1,0:T(8,128)S(1)}, f32[1,1]{1,0:T(1,128)}) custom-call(bf16[16,512]{1,0:T(8,128)(2,1)} %t_in.1, bf16[16,512]{1,0:T(8,128)(2,1)} %s_in.1, bf16[16,4096]{1,0:T(8,128)(2,1)} %p_in.1), custom_call_target="tpu_custom_call" | custom-call | tf_op jit(solution)/shard_map/pallas_call | solution.py:514
  93.7 0.7 copy.9
  94.4 0.6 copy.10

commit v5 on v4

--- a/solution.py
+++ b/solution.py
@@ -20,10 +20,21 @@
 QUART = COLS // 4
 NEAR = (2, 1, 3)
 LAG = 5
+RELAYED = (0, 1, 2)
 CROPS = ROWS * SIDE * SIDE
 WIRE_TOP = 8192.0
 CROP_SCALE = WIRE_TOP * (CROPS * STUDENT_TEMP) / 2.1
 MSGW = CHUNK + 128
+
+
+def hops(step, size):
+    return min(step, size - step)
+
+
+BATCH_STEPS = sorted(
+    ((dy, dx) for dy in range(SIDE) for dx in range(SIDE) if dy or dx), key=lambda s: -hops(s[0], SIDE) - hops(s[1], SIDE)
+)
+PROTO_STEPS = sorted(((dz, dc) for dz in range(8) for dc in range(2) if dz or dc), key=lambda s: -2 * hops(s[0], 8) - s[1])
 
 SCRATCH = dict(
     praw=((K, COLS), BF16),
@@ -67,8 +78,8 @@
     own=(3,),
     ag1_s=(4, 3),
     ag1_r=(4, 3),
-    ag2_s=(4, 4, 3),
-    ag2_r=(4, 4, 3),
+    ag2_s=(4, 4, 4),
+    ag2_r=(4, 4, 4),
     ts_s=(2, 16),
     ts_r=(2, 16),
     cx_s=(3, 15),
@@ -101,6 +112,12 @@
     def proto_dev(p):
         return (bi, p)
 
+    def batch_peer(step, sign):
+        return (yi + SIDE + sign * step[0]) % SIDE * SIDE + (xi + SIDE + sign * step[1]) % SIDE
+
+    def proto_peer(step, sign):
+        return (zi + 8 + sign * step[0]) % 8 * 2 + (ci + step[1]) % 2
+
     def rdma(src, dst, ssem, rsem, dev):
         return pltpu.make_async_remote_copy(
             src_ref=src, dst_ref=dst, send_sem=ssem, recv_sem=rsem, device_id=dev, device_id_type=MESH
@@ -111,15 +128,20 @@
         copy.start()
         started.append(copy)
 
+    def drain(count):
+        for copy in started[:count]:
+            copy.wait_send()
+        del started[:count]
+
     def arrived(dst, ssem, rsem, dev):
         rdma(dst, dst, ssem, rsem, dev).wait_recv()
 
     barrier = pltpu.get_barrier_semaphore()
     peers = []
-    for d in (8, 9, 7, 6, 10, 11, 5, 4, 12, 13, 3, 2, 14, 15, 1):
-        peers.append(proto_dev((pi + d) % NP))
-    for d in (10, 9, 11, 6, 14, 8, 2, 5, 7, 13, 15, 1, 3, 4, 12):
-        peers.append(((bi + d) % NP, pi))
+    for step in PROTO_STEPS:
+        peers.append(proto_dev(proto_peer(step, 1)))
+    for step in BATCH_STEPS:
+        peers.append((batch_peer(step, 1), pi))
     for peer in peers:
         pl.semaphore_signal(barrier, inc=1, device_id=peer, device_id_type=MESH)
     pl.semaphore_wait(barrier, len(peers))
@@ -135,6 +157,12 @@
 
     def piece(k, y, x):
         return m.praw.at[pl.ds(row0(y, x), BLK), pl.ds(k * QUART, QUART)]
+
+    def half_piece(k, y, x, half):
+        return m.praw.at[pl.ds(row0(y, x), BLK), pl.ds(k * QUART + half * (QUART // 2), QUART // 2)]
+
+    def second_steps(k):
+        return (1, 3) if k in RELAYED else NEAR
 
     own = [
         pltpu.make_async_copy(p_in, m.praw.at[pl.ds(row0(yi, xi), BLK), :], m.own.at[0]),
@@ -149,7 +177,7 @@
             send(p_in.at[:, pl.ds(k * QUART, QUART)], piece(k, yi, xi), m.ag1_s.at[k, d - 1], m.ag1_r.at[k, d - 1], to)
     for k in range(4):
         i1, i2 = pos[k % 2]
-        for d in NEAR:
+        for d in second_steps(k):
             to = batch_dev(*where(k % 2, i1, i2 + d))
             send(p_in.at[:, pl.ds(k * QUART, QUART)], piece(k, yi, xi), m.ag2_s.at[k, 0, d - 1], m.ag2_r.at[k, 0, d - 1], to)
 
@@ -173,7 +201,7 @@
             y, x = where(h, i1 - d, i2)
             block = piece(k, y, x)
             arrived(block, m.ag1_s.at[k, d - 1], m.ag1_r.at[k, d - 1], batch_dev(y, x))
-            for d2 in NEAR:
+            for d2 in second_steps(k):
                 send(block, block, m.ag2_s.at[k, d, d2 - 1], m.ag2_r.at[k, d, d2 - 1], batch_dev(*where(h, i1, i2 + d2)))
 
     def ts_forward(a):
@@ -193,6 +221,17 @@
             arrived(rows, m.ts_s.at[a, 7 + d], m.ts_r.at[a, 7 + d], proto_dev(sibling))
 
     ts_forward(0)
+    for k in RELAYED:
+        h = k % 2
+        i1, i2 = pos[h]
+        for r in (0, 1, 3, 2):
+            for half, d in enumerate((1, 3)):
+                y, x = where(h, i1 - r, i2 - d)
+                block = piece(k, y, x)
+                arrived(block, m.ag2_s.at[k, r, d - 1], m.ag2_r.at[k, r, d - 1], batch_dev(y, x))
+                block = half_piece(k, y, x, half)
+                slot = 1 + 2 * half
+                send(block, block, m.ag2_s.at[k, r, slot], m.ag2_r.at[k, r, slot], batch_dev(*where(h, i1, i2 + d)))
     ts_forward(1)
 
     def unit(values):
@@ -233,6 +272,12 @@
         h = k % 2
         i1, i2 = pos[h]
         for r in range(4):
+            if k in RELAYED:
+                y, x = where(h, i1 - r, i2 - 2)
+                for half in range(2):
+                    slot = 1 + 2 * half
+                    arrived(half_piece(k, y, x, half), m.ag2_s.at[k, r, slot], m.ag2_r.at[k, r, slot], batch_dev(y, x))
+                continue
             for d in (1, 3, 2):
                 y, x = where(h, i1 - r, i2 - d)
                 arrived(piece(k, y, x), m.ag2_s.at[k, r, d - 1], m.ag2_r.at[k, r, d - 1], batch_dev(y, x))
@@ -240,13 +285,13 @@
     to_message(m.cx.at[0, bi])
 
     def all_send(buf, ss, rs):
-        for d in range(1, NP):
-            send(buf.at[bi], buf.at[bi], ss.at[d - 1], rs.at[d - 1], ((bi + d) % NP, pi))
+        for n, step in enumerate(BATCH_STEPS):
+            send(buf.at[bi], buf.at[bi], ss.at[n], rs.at[n], (batch_peer(step, 1), pi))
 
     def all_sum(buf, ss, rs):
-        for d in range(1, NP):
-            frm = (bi + NP - d) % NP
-            arrived(buf.at[frm], ss.at[d - 1], rs.at[d - 1], (frm, pi))
+        for n, step in reversed(list(enumerate(BATCH_STEPS))):
+            frm = batch_peer(step, -1)
+            arrived(buf.at[frm], ss.at[n], rs.at[n], (frm, pi))
         return jnp.sum(buf[...], axis=0)
 
     def message(e):
@@ -275,13 +320,13 @@
         return batch_dev(y, xi)
 
     def row_start(e):
-        for d in range(1, NP):
-            send(m.rx.at[e, pi], m.rx.at[e, pi], m.rx_s.at[e, d - 1], m.rx_r.at[e, d - 1], proto_dev((pi + d) % NP))
+        for n, step in enumerate(PROTO_STEPS):
+            send(m.rx.at[e, pi], m.rx.at[e, pi], m.rx_s.at[e, n], m.rx_r.at[e, n], proto_dev(proto_peer(step, 1)))
 
     def row_finish(e):
-        for d in range(1, NP):
-            frm = (pi + NP - d) % NP
-            arrived(m.rx.at[e, frm], m.rx_s.at[e, d - 1], m.rx_r.at[e, d - 1], proto_dev(frm))
+        for n, step in reversed(list(enumerate(PROTO_STEPS))):
+            frm = proto_peer(step, -1)
+            arrived(m.rx.at[e, frm], m.rx_s.at[e, n], m.rx_r.at[e, n], proto_dev(frm))
         return jnp.sum(m.rx[e], axis=0)
 
     def to_rows(acc_ref, e, first):
@@ -309,6 +354,7 @@
 
     lax.fori_loop(0, NCHUNK, student_chunk, 0)
     to_rows(m.rowacc, 0, 4)
+    drain(len(started) - 15)
 
     def row_pass(e):
         def step(r, carry):
@@ -342,6 +388,7 @@
         if e:
             col_pass(e)
             col_start(e)
+            drain(len(started) - 15)
         sums = col_finish(e)
         total = sums[:, :CHUNK]
         if e == 1:
@@ -358,6 +405,7 @@
             m.rx[2, pi, 6:8, :] = mass
         row_pass(e)
         row_start(e)
+        drain(len(started) - 15)
         rows = row_finish(e)
         to_columns(m.csb, 1.0 / rows[0:4])
         if e == 0:
@@ -485,6 +533,7 @@
     all_send(m.lx, m.l_s, m.l_r)
     for j in range(NCHUNK - LAG + 2, NCHUNK):
         second_send(j)
+    drain(len(started) - 12)
     dots = ring_sum(m.dy, yi, along_y, m.d_s.at[1], m.d_r.at[1])
 
     loss_out[0, 0] = jnp.sum(all_sum(m.lx, m.l_s, m.l_r)[0:1]) * (-1.0 / CROPS)
@@ -504,8 +553,7 @@
         proto_own = m.pu[proto_rows, cols].astype(F32)
         gp_out[:, cols] = (reduced(j) - proto_own * dots[j : j + 1]) * m.pscale[:, cols]
 
-    for copy in started:
-        copy.wait_send()
+    drain(len(started))
 
 
 def shards(teacher_emb, student_emb, prototypes):

time: 97.5 us -> 93.9 us (0.963)
  Pallas kernels: 93.1 us -> 89.8 us
    pallas_call x1, Pallas kernels: 93.1 us -> 89.8 us  [shards(): pl.pallas_call(body, out_shape=(pltpu.VMEM((BLK, COLS), F32), pltpu.VMEM(...]
where the time goes in v5:
time: 93.9 us; the launch traced here: 93.5 us
  Pallas kernels  89.8 us (96%)
  between operations  2.33 us (2%)
  local copies, waits for them, and re-layouts  1.32 us (1%)
    pallas_call x1, Pallas kernels, shards(): pl.pallas_call(body, out_shape=(pltpu.VMEM((BLK, COLS), F32), pltpu.VMEM(...  89.8 us

profile of v5, /device:TPU:2, one launch (start us, length us, event | category | flops | bytes accessed | tf_op | source)
XLA Modules:
  0.0 93.5 jit_solution(6290490829946906953)
XLA Ops:
  0.6 89.8 %shard_map.58 = (f32[16,4096]{1,0:T(8,128)S(1)}, f32[16,512]{1,0:T(8,128)S(1)}, f32[1,1]{1,0:T(1,128)}) custom-call(bf16[16,512]{1,0:T(8,128)(2,1)} %t_in.1, bf16[16,512]{1,0:T(8,128)(2,1)} %s_in.1, bf16[16,4096]{1,0:T(8,128)(2,1)} %p_in.1), custom_call_target="tpu_custom_call" | custom-call | tf_op jit(solution)/shard_map/pallas_call | solution.py:562
  90.5 0.7 copy.9
  91.2 0.6 copy.10

commit v6 on v5

--- a/solution.py
+++ b/solution.py
@@ -139,9 +139,11 @@
     barrier = pltpu.get_barrier_semaphore()
     peers = []
     for step in PROTO_STEPS:
-        peers.append(proto_dev(proto_peer(step, 1)))
+        if step[1] == 0 or step[0] == 0:
+            peers.append(proto_dev(proto_peer(step, 1)))
     for step in BATCH_STEPS:
-        peers.append((batch_peer(step, 1), pi))
+        if step[0] == 0 or step[1] == 0:
+            peers.append((batch_peer(step, 1), pi))
     for peer in peers:
         pl.semaphore_signal(barrier, inc=1, device_id=peer, device_id_type=MESH)
     pl.semaphore_wait(barrier, len(peers))

time: 93.9 us -> 92.6 us (0.986)
  Pallas kernels: 89.8 us -> 88.8 us
    pallas_call x1, Pallas kernels: 89.8 us -> 88.8 us  [shards(): pl.pallas_call(body, out_shape=(pltpu.VMEM((BLK, COLS), F32), pltpu.VMEM(...]
where the time goes in v6:
time: 92.6 us; the launch traced here: 92.5 us
  Pallas kernels  88.8 us (96%)
  between operations  2.33 us (3%)
  local copies, waits for them, and re-layouts  1.32 us (1%)
    pallas_call x1, Pallas kernels, shards(): pl.pallas_call(body, out_shape=(pltpu.VMEM((BLK, COLS), F32), pltpu.VMEM(...  88.8 us

profile of v6, /device:TPU:2, one launch (start us, length us, event | category | flops | bytes accessed | tf_op | source)
XLA Modules:
  0.0 92.5 jit_solution(11907257484043660225)
XLA Ops:
  0.6 88.8 %shard_map.58 = (f32[16,4096]{1,0:T(8,128)S(1)}, f32[16,512]{1,0:T(8,128)S(1)}, f32[1,1]{1,0:T(1,128)}) custom-call(bf16[16,512]{1,0:T(8,128)(2,1)} %t_in.1, bf16[16,512]{1,0:T(8,128)(2,1)} %s_in.1, bf16[16,4096]{1,0:T(8,128)(2,1)} %p_in.1), custom_call_target="tpu_custom_call" | custom-call | tf_op jit(solution)/shard_map/pallas_call | solution.py:564
  89.5 0.7 copy.9
  90.2 0.6 copy.10

commit v7 on v6

--- a/solution.py
+++ b/solution.py
@@ -73,6 +73,7 @@
     s2=((NCHUNK, 3, BLK, CHUNK), BF16),
     r2=((NCHUNK, 3, BLK, CHUNK), BF16),
     smax=((8, CHUNK), F32),
+    prob=((ROWS, COLS), F32),
 )
 SEMS = dict(
     own=(3,),
@@ -364,7 +365,10 @@
             acc = jnp.zeros((8, 8, 128), F32)
             for q in range(COLS // 128):
                 cols = slice(q * 128, (q + 1) * 128)
-                acc = acc + m.expo[rows, cols].reshape(8, 8, 128) * m.pinv[:, cols]
+                product = m.expo[rows, cols].reshape(8, 8, 128) * m.pinv[:, cols]
+                if e == 2:
+                    m.expo[rows, cols] = product.reshape(64, 128)
+                acc = acc + product
             m.rowacc[rows, :] = acc.reshape(64, 128)
             return carry
 
@@ -391,6 +395,16 @@
             col_pass(e)
             col_start(e)
             drain(len(started) - 15)
+            if e == 2:
+                def softmax_step(r, carry):
+                    rows = pl.ds(pl.multiple_of(r * 64, 64), 64)
+                    inv = m.itot[rows, :]
+                    for q in range(COLS // 128):
+                        cols = slice(q * 128, (q + 1) * 128)
+                        m.prob[rows, cols] = jnp.exp2(m.cos[rows, cols] * (LOG2E / STUDENT_TEMP)) * inv
+                    return carry
+
+                lax.fori_loop(0, ROWS // 64, softmax_step, 0)
         sums = col_finish(e)
         total = sums[:, :CHUNK]
         if e == 1:
@@ -438,13 +452,13 @@
 
         def rows_step(r, inner):
             rows = pl.ds(pl.multiple_of(r * 64, 64), 64)
-            weights, inv = m.csb[rows, :], m.itot[rows, :]
+            weights = m.csb[rows, :]
             tl = jnp.zeros((64, 128), F32)
             for i in range(4):
                 sub = pl.ds(j * CHUNK + i * 128, 128)
-                target = (m.expo[rows, sub].reshape(8, 8, 128) * m.pinv[:, sub]).reshape(64, 128) * weights
+                target = m.expo[rows, sub] * weights
                 c = m.cos[rows, sub]
-                prob = jnp.exp2(c * (LOG2E / STUDENT_TEMP)) * inv
+                prob = m.prob[rows, sub]
                 tl = tl + target * c
                 m.gl[rows, i * 128 : (i + 1) * 128] = ((prob - target) * (1.0 / (CROPS * STUDENT_TEMP))).astype(BF16)
             m.tlacc[...] += jnp.sum(tl.reshape(8, 8, 128), axis=0)

time: 92.6 us -> 92.4 us (level)
  no operation moved by 1% of the time
where the time goes in v7:
time: 92.4 us; the launch traced here: 92.3 us
  Pallas kernels  88.7 us (96%)
  between operations  2.33 us (3%)
  local copies, waits for them, and re-layouts  1.32 us (1%)
    pallas_call x1, Pallas kernels, shards(): pl.pallas_call(body, out_shape=(pltpu.VMEM((BLK, COLS), F32), pltpu.VMEM(...  88.7 us

profile of v7, /device:TPU:2, one launch (start us, length us, event | category | flops | bytes accessed | tf_op | source)
XLA Modules:
  0.0 92.3 jit_solution(13017412563767149848)
XLA Ops:
  0.6 88.7 %shard_map.58 = (f32[16,4096]{1,0:T(8,128)S(1)}, f32[16,512]{1,0:T(8,128)S(1)}, f32[1,1]{1,0:T(1,128)}) custom-call(bf16[16,512]{1,0:T(8,128)(2,1)} %t_in.1, bf16[16,512]{1,0:T(8,128)(2,1)} %s_in.1, bf16[16,4096]{1,0:T(8,128)(2,1)} %p_in.1), custom_call_target="tpu_custom_call" | custom-call | tf_op jit(solution)/shard_map/pallas_call | solution.py:578
  89.3 0.7 copy.9
  90.0 0.6 copy.10

commit v8 on v7

--- a/solution.py
+++ b/solution.py
@@ -53,7 +53,6 @@
     pinv=((8, COLS), F32),
     csb=((ROWS, 128), F32),
     itot=((ROWS, 128), F32),
-    tlacc=((8, 128), F32),
     gl=((ROWS, CHUNK), BF16),
     gp=((K, COLS), F32),
     cg=((K, ROWS), F32),
@@ -422,6 +421,17 @@
         row_pass(e)
         row_start(e)
         drain(len(started) - 15)
+        if e == 2:
+            def loss_step(r, carry):
+                rows = pl.ds(pl.multiple_of(r * 64, 64), 64)
+                acc = jnp.zeros((64, 128), F32)
+                for q in range(COLS // 128):
+                    cols = slice(q * 128, (q + 1) * 128)
+                    acc = acc + m.expo[rows, cols] * m.cos[rows, cols]
+                m.rowacc[rows, :] = acc
+                return carry
+
+            lax.fori_loop(0, ROWS // 64, loss_step, 0)
         rows = row_finish(e)
         to_columns(m.csb, 1.0 / rows[0:4])
         if e == 0:
@@ -444,7 +454,9 @@
         root = jnp.exp2(jnp.log(jnp.maximum(jnp.abs(coded), 1e-37)) * (-8.0 / 9.0 * LOG2E))
         return (coded * root) * unscale
 
-    m.tlacc[...] = jnp.zeros_like(m.tlacc)
+    loss_rows = jnp.sum(m.csb[...] * m.rowacc[...], axis=0, keepdims=True) * (1.0 / STUDENT_TEMP)
+    m.lx[bi] = jnp.broadcast_to(loss_rows - log_total * (1.0 / NP), (8, 128))
+
     m.cg[...] = jnp.zeros_like(m.cg)
 
     def grad_chunk(j, carry):
@@ -453,15 +465,11 @@
         def rows_step(r, inner):
             rows = pl.ds(pl.multiple_of(r * 64, 64), 64)
             weights = m.csb[rows, :]
-            tl = jnp.zeros((64, 128), F32)
             for i in range(4):
                 sub = pl.ds(j * CHUNK + i * 128, 128)
                 target = m.expo[rows, sub] * weights
-                c = m.cos[rows, sub]
                 prob = m.prob[rows, sub]
-                tl = tl + target * c
                 m.gl[rows, i * 128 : (i + 1) * 128] = ((prob - target) * (1.0 / (CROPS * STUDENT_TEMP))).astype(BF16)
-            m.tlacc[...] += jnp.sum(tl.reshape(8, 8, 128), axis=0)
             return inner
 
         lax.fori_loop(0, ROWS // 64, rows_step, 0)
@@ -517,6 +525,8 @@
     for j in range(NCHUNK):
         grad_chunk(j, 0)
         first_send(j)
+        if j == 0:
+            all_send(m.lx, m.l_s, m.l_r)
         if j >= LAG:
             second_send(j - LAG)
     for p in range(NP):
@@ -526,7 +536,7 @@
     for q in range(4):
         m.rx[3, pi, q : q + 1, :] = dot_rows[:, q * 128 : (q + 1) * 128]
     m.rx[3, pi, 4:8, :] = jnp.zeros((4, 128), F32)
-    m.rx[3, pi, 4:5, :] = jnp.sum(m.tlacc[...], axis=0, keepdims=True)
+    m.rx[3, pi, 4:5, :] = all_sum(m.lx, m.l_s, m.l_r)[0:1]
     row_start(3)
     to_message(m.dx.at[xi])
     ring_send(m.dx, xi, along_x, m.d_s.at[0], m.d_r.at[0])
@@ -543,16 +553,13 @@
     ring_send(m.dy, yi, along_y, m.d_s.at[1], m.d_r.at[1])
     second_send(NCHUNK - LAG + 1)
 
-    rows = row_finish(3)
-    loss_rows = rows[4:5] * (1.0 / STUDENT_TEMP) - log_total
-    m.lx[bi] = jnp.broadcast_to(loss_rows, (8, 128))
-    all_send(m.lx, m.l_s, m.l_r)
     for j in range(NCHUNK - LAG + 2, NCHUNK):
         second_send(j)
     drain(len(started) - 12)
     dots = ring_sum(m.dy, yi, along_y, m.d_s.at[1], m.d_r.at[1])
 
-    loss_out[0, 0] = jnp.sum(all_sum(m.lx, m.l_s, m.l_r)[0:1]) * (-1.0 / CROPS)
+    rows = row_finish(3)
+    loss_out[0, 0] = jnp.sum(rows[4:5]) * (-1.0 / CROPS)
     crop_part = m.cgm[zi]
     for d in range(1, 8):
         frm = (zi + 8 - d) % 8

time: 92.4 us -> 92.1 us (level)
  no operation moved by 1% of the time
where the time goes in v8:
time: 92.1 us; the launch traced here: 91.7 us
  Pallas kernels  88 us (96%)
  between operations  2.33 us (3%)
  local copies, waits for them, and re-layouts  1.32 us (1%)
    pallas_call x1, Pallas kernels, shards(): pl.pallas_call(body, out_shape=(pltpu.VMEM((BLK, COLS), F32), pltpu.VMEM(...  88 us

profile of v8, /device:TPU:2, one launch (start us, length us, event | category | flops | bytes accessed | tf_op | source)
XLA Modules:
  0.0 91.7 jit_solution(2875092022603271391)
XLA Ops:
  0.6 88.0 %shard_map.58 = (f32[16,4096]{1,0:T(8,128)S(1)}, f32[16,512]{1,0:T(8,128)S(1)}, f32[1,1]{1,0:T(1,128)}) custom-call(bf16[16,512]{1,0:T(8,128)(2,1)} %t_in.1, bf16[16,512]{1,0:T(8,128)(2,1)} %s_in.1, bf16[16,4096]{1,0:T(8,128)(2,1)} %p_in.1), custom_call_target="tpu_custom_call" | custom-call | tf_op jit(solution)/shard_map/pallas_call | solution.py:585
  88.6 0.7 copy.9
  89.3 0.6 copy.10
